TPU v7x, 256 devices: a whole 4x4x8 slice. The times are simulated.
256 devices in a mesh: pipe: 4 (over y), expert: 16 (over z_lo, x), dp: 4 (over z_hi, core).
Axes of the slice: x: 4, y: 4, z: 8 (z_hi: 2, z_lo: 4; z = z_hi * 4 + z_lo), core: 2. Of those that a mesh axis runs over, the one named last changes fastest.
Arguments:
- fwd_in: bfloat16 [4, 2048, 3584], P('pipe', 'expert'), may hold values from -6 to 6
- fwd_routes: int32 [4, 2048, 2], P('pipe', 'expert'), may hold values from 0 to 15, all different within a row; in each aligned block of 128 rows (0 to 127, 128 to 255, ..., all dimensions but the last counted through in order) at most 20 rows name the same one
- fwd_weights: float32 [4, 2048, 2], P('pipe', 'expert'), may hold values from 0.05 to 0.5
- bwd_saved: bfloat16 [4, 2048, 3584], P('pipe', 'expert'), may hold values from -6 to 6
- bwd_grad: bfloat16 [4, 2048, 3584], P('pipe', 'expert'), may hold values from -6 to 6
- bwd_routes: int32 [4, 2048, 2], P('pipe', 'expert'), may hold values from 0 to 15, all different within a row; in each aligned block of 128 rows (0 to 127, 128 to 255, ..., all dimensions but the last counted through in order) at most 20 rows name the same one
- bwd_weights: float32 [4, 2048, 2], P('pipe', 'expert'), may hold values from 0.05 to 0.5
- expert_gate: bfloat16 [4, 16, 3584, 1024], P('pipe', 'expert', None, 'dp'), may hold values from -0.09375 to 0.09375
- expert_up: bfloat16 [4, 16, 3584, 1024], P('pipe', 'expert', None, 'dp'), may hold values from -0.09375 to 0.09375
- expert_down: bfloat16 [4, 16, 1024, 3584], P('pipe', 'expert', 'dp'), may hold values from -0.1875 to 0.1875
Outputs:
- fwd_out: bfloat16 [4, 2048, 3584], P('pipe', 'expert')
- bwd_out: bfloat16 [4, 2048, 3584], P('pipe', 'expert')
Inputs may be any that keep to these rules, and one draw needn't show every extreme that they name: `fwd_routes`: A token names 2 different experts. In every section, the 128 tokens of one index of the expert axis (aligned blocks of rows) name no expert more than 20 times, a bound that some block reaches. `bwd_routes`: A token names 2 different experts. In every section, the 128 tokens of one index of the expert axis (aligned blocks of rows) name no expert more than 20 times, a bound that some block reaches.
All inputs are finite; a program needn't handle non-finite values.
Results may differ from a plain program's by a relative error of at most 0.02.
Values may be sent and summed in bfloat16 or wider, within the bound.
A program may use at most 128 MiB of HBM per device.

v0:
```python
import jax
import jax.numpy as jnp
from jax import lax
from jax.sharding import PartitionSpec as P

CAP = 20


def passed_along(value, axis, steps):
    count = lax.axis_size(axis)
    pairs = [(source, (source + steps) % count) for source in range(count)]
    return lax.ppermute(value, axis, pairs)


def route_slots(routes, experts_here, total, capacity):
    flat_ids = routes.reshape(-1)
    hits = (flat_ids[:, None] == jnp.arange(total, dtype=jnp.int32)[None, :]).astype(jnp.int32)
    ranks = jnp.sum((jnp.cumsum(hits, axis=0) - 1) * hits, axis=1)
    owners = flat_ids // experts_here
    within = flat_ids % experts_here
    return (owners * capacity + ranks) * experts_here + within


def spread_matrix(slot_ids, values, tok_count, top_count, slot_count):
    marks = (slot_ids[:, None] == jnp.arange(slot_count, dtype=jnp.int32)[None, :]).astype(
        jnp.float32
    )
    marks = marks * values[:, None]
    return jnp.sum(marks.reshape(tok_count, top_count, slot_count), axis=1)


def hidden_rows(piece, joint, half):
    pre = jnp.einsum("red,edh->reh", piece, joint, preferred_element_type=jnp.float32)
    return (jax.nn.silu(pre[..., :half]) * pre[..., half:]).astype(jnp.bfloat16)


def grad_rows(piece, joint, down, half):
    inputs = piece[:, :, 0]
    grads = piece[:, :, 1]
    pre = jnp.einsum("red,edh->reh", inputs, joint, preferred_element_type=jnp.float32)
    gate_pre = pre[..., :half]
    up_pre = pre[..., half:]
    back = jnp.einsum("red,ehd->reh", grads, down, preferred_element_type=jnp.float32)
    sigmoid_gate = jax.nn.sigmoid(gate_pre)
    d_gate = back * up_pre * sigmoid_gate * (1.0 + gate_pre * (1.0 - sigmoid_gate))
    d_up = back * jax.nn.silu(gate_pre)
    return jnp.concatenate([d_gate.astype(jnp.bfloat16), d_up.astype(jnp.bfloat16)], axis=-1)


def pick_rows(returned, slot_ids, tok_count, top_count):
    flat_rows = returned.reshape(-1, returned.shape[-1])
    picked = jnp.take(flat_rows, slot_ids, axis=0)
    return picked.reshape(tok_count, top_count, returned.shape[-1])


def body(
    fwd_in,
    fwd_routes,
    fwd_weights,
    bwd_saved,
    bwd_grad,
    bwd_routes,
    bwd_weights,
    expert_gate,
    expert_up,
    expert_down,
):
    experts_here = expert_gate.shape[1]
    width = expert_gate.shape[2]
    hid_dev = expert_gate.shape[3]
    experts_axis = lax.axis_size("expert")
    total = experts_axis * experts_here
    capacity = CAP
    slot_count = total * capacity
    tok_count = fwd_in.shape[1]
    top_count = fwd_routes.shape[2]
    joint_here = jnp.concatenate([expert_gate[0], expert_up[0]], axis=2)
    down_here = expert_down[0]
    saved_rows = bwd_saved[0]
    back_slots = route_slots(bwd_routes[0], experts_here, total, capacity)
    ones_flat = jnp.ones((tok_count * top_count,), jnp.float32)
    back_ones = spread_matrix(back_slots, ones_flat, tok_count, top_count, slot_count)
    back_marks = back_ones.astype(jnp.bfloat16)
    input_send = jnp.einsum("ts,td->sd", back_marks, saved_rows, preferred_element_type=jnp.float32)
    input_send = input_send.astype(jnp.bfloat16).reshape(
        experts_axis, capacity, experts_here, width
    )
    rows_in = passed_along(fwd_in[0], "pipe", 1)
    grads_in = passed_along(bwd_grad[0], "pipe", -1)
    fwd_slots = route_slots(fwd_routes[0], experts_here, total, capacity)
    fwd_ones = spread_matrix(fwd_slots, ones_flat, tok_count, top_count, slot_count)
    fwd_send = jnp.einsum(
        "ts,td->sd", fwd_ones.astype(jnp.bfloat16), rows_in, preferred_element_type=jnp.float32
    )
    fwd_send = fwd_send.astype(jnp.bfloat16).reshape(experts_axis, capacity, experts_here, width)
    received = lax.all_to_all(fwd_send, "expert", split_axis=0, concat_axis=1, tiled=True)[0]
    forward_hidden = hidden_rows(received, joint_here, hid_dev)
    forward_partial = jnp.einsum(
        "reh,ehd->red", forward_hidden, down_here, preferred_element_type=jnp.float32
    )
    forward_total = lax.psum(forward_partial.astype(jnp.bfloat16), "dp")
    returned = lax.all_to_all(
        forward_total[None], "expert", split_axis=1, concat_axis=0, tiled=True
    )
    picked = pick_rows(returned, fwd_slots, tok_count, top_count)
    routed_sum = jnp.einsum(
        "tk,tkd->td", fwd_weights[0], picked.astype(jnp.float32), precision=lax.Precision.HIGHEST
    )
    fwd_out = routed_sum.astype(jnp.bfloat16)[None]
    back_scaled = spread_matrix(
        back_slots, bwd_weights[0].reshape(-1), tok_count, top_count, slot_count
    )
    slot_scale = jnp.sum(back_scaled, axis=0)
    grad_copies = jnp.einsum("ts,td->sd", back_marks, grads_in, preferred_element_type=jnp.float32)
    grad_send = (
        (slot_scale[:, None] * grad_copies)
        .astype(jnp.bfloat16)
        .reshape(experts_axis, capacity, experts_here, width)
    )
    pair_send = jnp.stack([input_send, grad_send], axis=3)
    pairs = lax.all_to_all(pair_send, "expert", split_axis=0, concat_axis=1, tiled=True)[0]
    both_grads = grad_rows(pairs, joint_here, down_here, hid_dev)
    backward_partial = jnp.einsum(
        "reh,edh->red", both_grads, joint_here, preferred_element_type=jnp.float32
    )
    backward_total = lax.psum(backward_partial.astype(jnp.bfloat16), "dp")
    back_returned = lax.all_to_all(
        backward_total[None], "expert", split_axis=1, concat_axis=0, tiled=True
    )
    back_picked = pick_rows(back_returned, back_slots, tok_count, top_count)
    routed_grad = jnp.sum(back_picked.astype(jnp.float32), axis=1)
    bwd_out = routed_grad.astype(jnp.bfloat16)[None]
    return (fwd_out, bwd_out)


def solution(mesh):
    placed = (
        P("pipe", "expert", None),
        P("pipe", "expert", None),
        P("pipe", "expert", None),
        P("pipe", "expert", None),
        P("pipe", "expert", None),
        P("pipe", "expert", None),
        P("pipe", "expert", None),
        P("pipe", "expert", None, "dp"),
        P("pipe", "expert", None, "dp"),
        P("pipe", "expert", "dp", None),
    )
    return jax.shard_map(
        body,
        mesh=mesh,
        in_specs=placed,
        out_specs=(P("pipe", "expert", None), P("pipe", "expert", None)),
        check_vma=False,
    )
```

profile of v0, /device:TPU:64, one launch (start us, length us, event | category | flops | bytes accessed | tf_op | source)
XLA Modules:
  0.0 586.3 jit_solution(13822214034596646060)
XLA Ops:
  11.1 19.7 %collective-permute-done = bf16[128,3584]{1,0:T(8,128)(2,1)S(1)} collective-permute-done((bf16[128,3584]{1,0:T(8,128)(2,1)}, bf16[128,3584]{1,0:T(8,128)(2,1)S(1)}, u32[]{:S(2)}, u32[]{:S(2)}) %collective-permute-start) | collective-permute-done | bytes 917536 | tf_op jit(solution)/shard_map/ppermute | solution.py:12
  33.0 4.2 reshape.176
  37.1 8.2 %all-to-all-start = ((bf16[16,20,1,3584]{3,1,2,0:T(8,128)(2,1)}), bf16[16,20,1,3584]{3,1,2,0:T(8,128)(2,1)}, u32[]{:S(2)}, u32[]{:S(2)}) async-start(bf16[16,20,1,3584]{3,1,2,0:T(8,128)(2,1)} %bitcast.145), calls=%async_computation | async-start | bytes 5505024 | tf_op jit(solution)/shard_map/all_to_all | solution.py:96
  50.9 4.1 stack_reshape.6
  55.1 11.3 %collective-permute-done.1 = bf16[128,3584]{1,0:T(8,128)(2,1)} collective-permute-done((bf16[128,3584]{1,0:T(8,128)(2,1)}, bf16[128,3584]{1,0:T(8,128)(2,1)}, u32[]{:S(2)}, u32[]{:S(2)}) %collective-permute-start.1) | collective-permute-done | bytes 917536 | tf_op jit(solution)/shard_map/ppermute | solution.py:12
  66.4 3.3 fusion
  69.7 4.1 stack_reshape.7
  73.8 5.6 pad_maximum_fusion
  79.4 9.4 %copy.73 = bf16[16,20,1,2,3584]{4,3,2,1,0:T(2,128)(2,1)} copy(bf16[16,20,1,2,3584]{4,1,0,3,2:T(8,128)(2,1)} %pad_maximum_fusion) | data formatting | bytes 9175040 | tf_op jit(solution)/shard_map/stack | solution.py:120
  88.8 18.1 %all-to-all-done = bf16[16,20,1,3584]{3,1,2,0:T(8,128)(2,1)} async-done(((bf16[16,20,1,3584]{3,1,2,0:T(8,128)(2,1)}), bf16[16,20,1,3584]{3,1,2,0:T(8,128)(2,1)}, u32[]{:S(2)}, u32[]{:S(2)}) %all-to-all-start) | async-done | bytes 2293792 | tf_op jit(solution)/shard_map/all_to_all | solution.py:96
  106.9 5.1 all-to-all-start.2
  112.3 4.2 reshape.177
  116.5 4.1 convolution_bitcast_fusion
  122.7 90.3 %all-to-all-done.2 = bf16[16,20,1,2,3584]{4,3,2,1,0:T(2,128)(2,1)} async-done(((bf16[16,20,1,2,3584]{4,3,2,1,0:T(2,128)(2,1)}), bf16[16,20,1,2,3584]{4,3,2,1,0:T(2,128)(2,1)}, u32[]{:S(2)}, u32[]{:S(2)}) %all-to-all-start.2) | async-done | bytes 4587552 | tf_op jit(solution)/shard_map/all_to_all | solution.py:121
  213.0 9.7 %fusion.42 = (bf16[320,1,1,3584]{3,2,0,1:T(2,128)(2,1)S(1)}, bf16[320,1,1,3584]{3,2,0,1:T(2,128)(2,1)S(1)}) fusion(bf16[320,1,2,3584]{3,2,0,1:T(2,128)(2,1)} %bitcast.25), kind=kLoop, calls=%fused_computation.78 | loop fusion | bytes 9175040 | tf_op jit(solution)/shard_map/slice | solution.py:38
  227.7 177.6 %all-reduce.3.cloned.1.call-done = (bf16[1,320,1,3584]{3,1,2,0:T(8,128)(2,1)}, bf16[1,320,1,3584]{3,1,2,0:T(8,128)(2,1)}) async-done(((bf16[1,320,1,3584]{3,1,2,0:T(8,128)(2,1)}, bf16[1,320,1,3584]{3,1,2,0:T(8,128)(2,1)}), (bf16[1,320,1,3584]{3,1,2,0:T(8,128)(2,1)}, bf16[1,320,1,3584]{3,1,2,0:T(8,128)(2,1)})) %all-reduce.3.cloned.1.call-update) | async-done | bytes 4587536 | tf_op jit(solution)/shard_map/psum | solution.py:101
  405.3 7.2 %copy.110 = bf16[1,320,1,3584]{3,2,0,1:T(2,128)(2,1)} copy(bf16[1,320,1,3584]{3,1,2,0:T(8,128)(2,1)} %get-tuple-element.5) | data formatting | bytes 4587520 | tf_op jit(solution)/shard_map/psum | solution.py:101
  413.0 14.4 %reduce.6 = bf16[320,3584]{1,0:T(8,128)(2,1)S(1)} reduce(bf16[320,1,1,3584]{3,2,1,0:T(2,128)(2,1)} %bitcast.141, bf16[]{:T(256)} %broadcast.222), dimensions={1,2}, to_apply=%bitcast.138.reduce_sub_computation | reduce | bytes 4587522
  429.9 8.1 %all-to-all-start.1 = ((bf16[16,2,35840]{2,1,0:T(2,128)(2,1)}), bf16[16,2,35840]{2,1,0:T(2,128)(2,1)S(1)}, u32[]{:S(2)}, u32[]{:S(2)}) async-start(bf16[16,2,35840]{2,1,0:T(2,128)(2,1)} %reshape.214), calls=%async_computation.1 | async-start | bytes 4587520 | tf_op jit(solution)/shard_map/all_to_all | solution.py:102
  438.0 7.2 %copy.109 = bf16[1,320,1,3584]{3,2,0,1:T(2,128)(2,1)} copy(bf16[1,320,1,3584]{3,1,2,0:T(8,128)(2,1)} %get-tuple-element.6) | data formatting | bytes 4587520 | tf_op jit(solution)/shard_map/psum | solution.py:126
  445.2 15.8 %reduce.7 = bf16[320,3584]{1,0:T(8,128)(2,1)} reduce(bf16[320,1,1,3584]{3,2,1,0:T(2,128)(2,1)} %bitcast.142, bf16[]{:T(256)} %broadcast.222), dimensions={1,2}, to_apply=%bitcast.137.reduce_sub_computation | reduce | bytes 4587522
  461.0 4.3 reshape.216
  465.3 25.4 %all-to-all-done.1 = bf16[16,2,35840]{2,1,0:T(2,128)(2,1)S(1)} async-done(((bf16[16,2,35840]{2,1,0:T(2,128)(2,1)}), bf16[16,2,35840]{2,1,0:T(2,128)(2,1)S(1)}, u32[]{:S(2)}, u32[]{:S(2)}) %all-to-all-start.1) | async-done | bytes 2293792 | tf_op jit(solution)/shard_map/all_to_all | solution.py:102
  490.7 5.6 all-to-all-start.3
  496.5 6.7 %reshape.215 = bf16[320,1,1,3584]{3,2,1,0:T(2,128)(2,1)} reshape(bf16[16,2,35840]{2,1,0:T(2,128)(2,1)S(1)} %all-to-all-done.1) | data formatting | bytes 4587520
  505.8 3.0 gather_fusion
  512.1 7.4 %fusion.43 = bf16[128,1,3584]{2,1,0:T(2,128)(2,1)S(1)} fusion(bf16[128,2,3584]{2,1,0:T(2,128)(2,1)} %reshape.181, f32[128,2,1]{1,2,0:T(1,128)S(1)} %copy.75), kind=kOutput, calls=%fused_computation.81 | convolution fusion | flops 11010048 | bytes 2753536 | tf_op jit(solution)/shard_map/tk,tkd->td/dot_general | solution.py:106
  520.6 27.3 %all-to-all-done.3 = bf16[16,2,35840]{2,1,0:T(2,128)(2,1)} async-done(((bf16[16,2,35840]{2,1,0:T(2,128)(2,1)}), bf16[16,2,35840]{2,1,0:T(2,128)(2,1)}, u32[]{:S(2)}, u32[]{:S(2)}) %all-to-all-start.3) | async-done | bytes 2293792 | tf_op jit(solution)/shard_map/all_to_all | solution.py:127
  547.9 10.4 %reshape.217 = bf16[320,1,1,3584]{3,2,1,0:T(2,128)(2,1)} reshape(bf16[16,2,35840]{2,1,0:T(2,128)(2,1)} %all-to-all-done.3) | data formatting | bytes 4587520
  563.9 3.0 broadcast_select_fusion
  566.9 5.2 reshape.187
  572.1 6.9 %reduce_sum.72 = bf16[128,3584]{1,0:T(8,128)(2,1)} reduce(bf16[128,2,3584]{2,1,0:T(2,128)(2,1)} %reshape.187, bf16[]{:T(256)} %constant.77.clone.1), dimensions={1}, to_apply=%region_11.13 | reduce | flops 458752 | bytes 2752514 | tf_op jit(solution)/shard_map/reduce_sum | solution.py:131
  (65 shorter events, 34.6 us)
Async XLA Ops:
  7.2 113.4 %copy-start = (bf16[1,1,256,3584]{3,2,1,0:T(8,128)(2,1)S(1)}, bf16[1,1,256,3584]{3,2,1,0:T(8,128)(2,1)}, u32[]{:S(2)}) copy-start(bf16[1,1,256,3584]{3,2,1,0:T(8,128)(2,1)} %param.21) | copy-start | bytes 5505028
  7.2 23.7 %collective-permute-start = (bf16[128,3584]{1,0:T(8,128)(2,1)}, bf16[128,3584]{1,0:T(8,128)(2,1)S(1)}, u32[]{:S(2)}, u32[]{:S(2)}) collective-permute-start(bf16[128,3584]{1,0:T(8,128)(2,1)} %bitcast.156), channel_id=1, source_target_pairs={{0,64},{64,128},{128,192},{192,0},{1,65},{65,129},{129,193},{193,1... | collective-permute-start | bytes 2752520 | tf_op jit(solution)/shard_map/ppermute | solution.py:12
  37.1 9.9 %copy-start.3 = (s32[1,128,2]{1,2,0:T(2,128)S(1)}, s32[1,128,2]{1,2,0:T(2,128)}, u32[]{:S(2)}) copy-start(s32[1,128,2]{1,2,0:T(2,128)} %param.17) | copy-start | bytes 3076
  37.1 11.5 %copy-start.4 = (f32[1,128,2]{1,2,0:T(2,128)S(1)}, f32[1,128,2]{1,2,0:T(2,128)}, u32[]{:S(2)}) copy-start(f32[1,128,2]{1,2,0:T(2,128)} %param.18) | copy-start | bytes 3076
  37.1 11.6 %copy-start.2 = (bf16[1,128,3584]{2,1,0:T(8,128)(2,1)S(1)}, bf16[1,128,3584]{2,1,0:T(8,128)(2,1)}, u32[]{:S(2)}) copy-start(bf16[1,128,3584]{2,1,0:T(8,128)(2,1)} %param.15) | copy-start | bytes 2752516
  37.1 69.8 %all-to-all-start = ((bf16[16,20,1,3584]{3,1,2,0:T(8,128)(2,1)}), bf16[16,20,1,3584]{3,1,2,0:T(8,128)(2,1)}, u32[]{:S(2)}, u32[]{:S(2)}) async-start(bf16[16,20,1,3584]{3,1,2,0:T(8,128)(2,1)} %bitcast.145), calls=%async_computation | async-start | bytes 5505024 | tf_op jit(solution)/shard_map/all_to_all | solution.py:96
  45.3 21.0 %collective-permute-start.1 = (bf16[128,3584]{1,0:T(8,128)(2,1)}, bf16[128,3584]{1,0:T(8,128)(2,1)}, u32[]{:S(2)}, u32[]{:S(2)}) collective-permute-start(bf16[128,3584]{1,0:T(8,128)(2,1)} %bitcast.157), channel_id=1, source_target_pairs={{0,192},{64,0},{128,64},{192,128},{1,193},{65,1},{129,65},{193,129... | collective-permute-start | bytes 2752520 | tf_op jit(solution)/shard_map/ppermute | solution.py:12
  106.9 106.1 %all-to-all-start.2 = ((bf16[16,20,1,2,3584]{4,3,2,1,0:T(2,128)(2,1)}), bf16[16,20,1,2,3584]{4,3,2,1,0:T(2,128)(2,1)}, u32[]{:S(2)}, u32[]{:S(2)}) async-start(bf16[16,20,1,2,3584]{4,3,2,1,0:T(2,128)(2,1)} %copy.73), calls=%async_computation.2 | async-start | bytes 9175040 | tf_op jit(solution)/shard_map/all_to_all | solution.py:121
  112.1 293.2 %all-reduce.3.cloned.1.call-start = ((), (), s32[]{:S(2)}) async-start(), calls=%async_computation.4 | async-start | bytes 9175040 | tf_op jit(solution)/shard_map/psum | solution.py:101
  213.0 9.7 %copy-start.6 = (bf16[1,1,3584,256]{3,2,1,0:T(8,128)(2,1)S(1)}, bf16[1,1,3584,256]{3,2,1,0:T(8,128)(2,1)}, u32[]{:S(2)}) copy-start(bf16[1,1,3584,256]{3,2,1,0:T(8,128)(2,1)} %param.20) | copy-start | bytes 5505028
  213.0 9.7 %copy-start.7 = (bf16[1,1,3584,256]{3,2,1,0:T(8,128)(2,1)S(1)}, bf16[1,1,3584,256]{3,2,1,0:T(8,128)(2,1)}, u32[]{:S(2)}) copy-start(bf16[1,1,3584,256]{3,2,1,0:T(8,128)(2,1)} %param.19) | copy-start | bytes 5505028
  429.9 60.9 %all-to-all-start.1 = ((bf16[16,2,35840]{2,1,0:T(2,128)(2,1)}), bf16[16,2,35840]{2,1,0:T(2,128)(2,1)S(1)}, u32[]{:S(2)}, u32[]{:S(2)}) async-start(bf16[16,2,35840]{2,1,0:T(2,128)(2,1)} %reshape.214), calls=%async_computation.1 | async-start | bytes 4587520 | tf_op jit(solution)/shard_map/all_to_all | solution.py:102
  465.3 31.0 %copy-start.5 = (f32[1,128,2]{1,2,0:T(2,128)S(1)}, f32[1,128,2]{1,2,0:T(2,128)}, u32[]{:S(2)}) copy-start(f32[1,128,2]{1,2,0:T(2,128)} %param.14) | copy-start | bytes 3076
  490.7 57.2 %all-to-all-start.3 = ((bf16[16,2,35840]{2,1,0:T(2,128)(2,1)}), bf16[16,2,35840]{2,1,0:T(2,128)(2,1)}, u32[]{:S(2)}, u32[]{:S(2)}) async-start(bf16[16,2,35840]{2,1,0:T(2,128)(2,1)} %reshape.216), calls=%async_computation.3 | async-start | bytes 4587520 | tf_op jit(solution)/shard_map/all_to_all | solution.py:127
  566.9 12.1 %copy-start.1 = (bf16[1,1,256,3584]{3,2,1,0:T(8,128)(2,1)S(1)}, bf16[1,1,256,3584]{3,2,1,0:T(8,128)(2,1)}, u32[]{:S(2)}) copy-start(bf16[1,1,256,3584]{3,2,1,0:T(8,128)(2,1)} %param.21) | copy-start | bytes 5505028
Sparse Core Ops, SparseCore 0:
  227.8 177.4 all-reduce.2
where the time goes:
time: 596 us; the launch traced here: 586 us
  waiting for transfers between devices  370 us (62%)
  local copies, waits for them, and re-layouts  95.9 us (16%)
  other arithmetic  49.1 us (8%)
  starting transfers between devices  30.6 us (5%)
  matrix products  26.2 us (4%)
  between operations  14.8 us (2%)
    psum x1, waiting for transfers between devices, body(): forward_total = lax.psum(forward_partial.astype(jnp.bfloat16), 'dp')  178 us
    all_to_all x1, waiting for transfers between devices, body(): lax.all_to_all(pair_send, 'expert', split_axis=0, concat_axis=1, tiled=True)  90.3 us
    ppermute x2, waiting for transfers between devices, passed_along(): return lax.ppermute(value, axis, pairs)  31 us
    unnamed x25, local copies, waits for them, and re-layouts  30.5 us
    unnamed x2, other arithmetic  30.2 us
    all_to_all x1, waiting for transfers between devices, body(): lax.all_to_all(backward_total[None], 'expert', split_axis=1, concat_axis=...  27.3 us
    all_to_all x1, waiting for transfers between devices, body(): lax.all_to_all(forward_total[None], 'expert', split_axis=1, concat_axis=0...  25.4 us
    all_to_all x1, waiting for transfers between devices, body(): lax.all_to_all(fwd_send, 'expert', split_axis=0, concat_axis=1, tiled=True)  18.1 us
  transfers between devices with their start and end apart: 7, of which 7 were waited for; matrix products, arithmetic and copies ran while one was open for 16% of the time, Pallas kernels for 0%

commit v1 on v0

v1 whole, which is shorter than its diff:
```python
import jax
import jax.numpy as jnp
from jax import lax
from jax.experimental import pallas as pl
from jax.experimental.pallas import tpu as pltpu
from jax.sharding import PartitionSpec as P

MESH = pl.DeviceIdType.MESH
BF16 = jnp.bfloat16
F32 = jnp.float32

BLOCKS = 8
STEP_Z = (0, 0, 1, 1, 2, -2, -1, -1)
CODE = 32
ROWS = BLOCKS * 16
SPARE = BLOCKS * 4
VMEM_LIMIT = 56 * 1024 * 1024


def place():
    pipe = lax.axis_index("pipe")
    expert = lax.axis_index("expert")
    dp = lax.axis_index("dp")
    return pipe, (dp // 2) * 4 + expert // 4, expert % 4, dp % 2


def step_x(k, core):
    return 2 * (k % 2) + (k // 2 + core) % 2


def device_of(pipe, ring, x, core):
    ring = (ring + 16) % 8
    x = (x + 8) % 4
    return ((pipe + 4) % 4, (ring % 4) * 4 + x, (ring // 4) * 2 + core)


def target_of(k, section):
    pipe, ring, x, core = place()
    return device_of(pipe + section, ring + STEP_Z[k], x + step_x(k, core), core)


def source_of(k, section):
    pipe, ring, x, core = place()
    return device_of(pipe + section, ring - STEP_Z[k], x - step_x(k, core), core)


def expert_of_block(b):
    _, ring, x, core = place()
    away = b >> 1
    return (((ring + away) & 3) << 2) + ((x + ((b & 1) << 1) + ((away + core) & 1)) & 3)


def dispatch_kernel(code_x, code_f, code_g, x_ref, f_ref, g_ref, gate, up, down,
                    got_x, got_f, got_g, gate2, up2, down2,
                    send_x, send_f, send_g, send_sem, recv_sem, wsend_sem, wrecv_sem, local_sem):
    pipe, ring, x, core = place()
    sibling = device_of(pipe, ring, x, 1 - core)
    sections = (0, 1, -1)
    quarter = x_ref.shape[1] // 4
    barrier = pltpu.get_barrier_semaphore()

    def greet(who):
        pl.semaphore_signal(barrier, inc=1, device_id=who, device_id_type=MESH)

    greet(sibling)
    for t in range(3):
        for k in range(BLOCKS):
            if t == 0 and k == 0:
                @pl.when(core == 1)
                def _():
                    greet(source_of(0, 0))
            else:
                greet(source_of(k, -sections[t]))

    row = lax.broadcasted_iota(jnp.int32, (ROWS, 1), 0)
    base = expert_of_block(row >> 4) * CODE
    near = base + (row & 15)
    over = base + 16 + (row & 3)
    part = (row >> 2) & 3

    def build(code_ref, rows_ref, send_ref):
        first, second = code_ref[0:1, :], code_ref[1:2, :]
        pick = jnp.where((first == near) | (second == near), 1.0, 0.0).astype(BF16)
        spare = jnp.where((first == over) | (second == over), 1.0, 0.0)
        total = jnp.zeros((ROWS, quarter), F32)
        for q in range(4):
            cols = rows_ref[:, q * quarter:(q + 1) * quarter]
            send_ref[:, q * quarter:(q + 1) * quarter] = jnp.dot(
                pick, cols, preferred_element_type=F32).astype(BF16)
            mine = jnp.where(part == q, spare, 0.0).astype(BF16)
            total = total + jnp.dot(mine, cols, preferred_element_type=F32)
        send_ref[:, 4 * quarter:] = total.astype(BF16)

    def copy(t, k):
        src = (send_x, send_f, send_g)[t]
        dst = (got_x, got_f, got_g)[t]
        return pltpu.make_async_remote_copy(
            src_ref=src.at[pl.ds(16 * k, 16)], dst_ref=dst.at[pl.ds(16 * k, 16)],
            send_sem=send_sem.at[t, k], recv_sem=recv_sem.at[t, k],
            device_id=target_of(k, sections[t]), device_id_type=MESH)

    def weight(i):
        return pltpu.make_async_remote_copy(
            src_ref=(gate, up, down)[i], dst_ref=(gate2, up2, down2)[i],
            send_sem=wsend_sem.at[i], recv_sem=wrecv_sem.at[i],
            device_id=sibling, device_id_type=MESH)

    own = pltpu.make_async_copy(send_x.at[pl.ds(0, 16)], got_x.at[pl.ds(0, 16)], local_sem)

    build(code_x, x_ref, send_x)

    @pl.when(core == 0)
    def _():
        pl.semaphore_wait(barrier, 3 * BLOCKS)

    @pl.when(core == 1)
    def _():
        pl.semaphore_wait(barrier, 3 * BLOCKS + 1)

    for t in range(3):
        if t == 1:
            build(code_f, f_ref, send_f)
        if t == 2:
            build(code_g, g_ref, send_g)
        for k in (4, 5, 2, 3, 6, 7, 1, 0):
            if t == 0 and k == 0:
                @pl.when(core == 0)
                def _():
                    own.start()

                @pl.when(core == 1)
                def _():
                    copy(0, 0).start()
            else:
                copy(t, k).start()
        weight(t).start()
    for t in range(3):
        for k in range(BLOCKS):
            if t == 0 and k == 0:
                @pl.when(core == 0)
                def _():
                    own.wait()

                @pl.when(core == 1)
                def _():
                    copy(0, 0).wait()
            else:
                copy(t, k).wait()
        weight(t).wait()


def dispatch(code_x, code_f, code_g, saved, fwd, grad, gate, up, down):
    width = saved.shape[1]
    packed = jax.ShapeDtypeStruct((ROWS, width + width // 4), BF16)
    vm = pl.BlockSpec(memory_space=pltpu.VMEM)
    hbm = pl.BlockSpec(memory_space=pl.ANY)
    return pl.pallas_call(
        dispatch_kernel,
        name="dispatch",
        out_shape=(packed,) * 3 + tuple(jax.ShapeDtypeStruct(w.shape, w.dtype) for w in (gate, up, down)),
        in_specs=[vm] * 6 + [hbm] * 3,
        out_specs=(hbm,) * 6,
        scratch_shapes=[pltpu.VMEM(packed.shape, BF16)] * 3 + [
            pltpu.SemaphoreType.DMA((3, BLOCKS)), pltpu.SemaphoreType.DMA((3, BLOCKS)),
            pltpu.SemaphoreType.DMA((3,)), pltpu.SemaphoreType.DMA((3,)), pltpu.SemaphoreType.DMA],
        compiler_params=pltpu.CompilerParams(
            collective_id=0, has_side_effects=True, vmem_limit_bytes=VMEM_LIMIT),
    )(code_x, code_f, code_g, saved, fwd, grad, gate, up, down)


def dot_nt(a, b):
    return lax.dot_general(a, b, (((1,), (1,)), ((), ())), preferred_element_type=F32)


def expert_kernel(got_x, got_f, got_g, gate, up, down, gate2, up2, down2, out_f, out_b,
                  left, left_g, pre, back, hid, dgate, dup, spare):
    width = gate.shape[0]
    half = gate.shape[1]
    quarter = width // 4
    rows = ROWS + SPARE
    a = lax.broadcasted_iota(jnp.int32, (SPARE, ROWS), 0)
    b = lax.broadcasted_iota(jnp.int32, (SPARE, ROWS), 1)
    fits = ((a >> 2) == (b >> 4)) & ((a & 3) == (b & 3))
    at = lax.broadcasted_iota(jnp.int32, (ROWS, SPARE), 0)
    bt = lax.broadcasted_iota(jnp.int32, (ROWS, SPARE), 1)
    fits_t = ((bt >> 2) == (at >> 4)) & ((bt & 3) == (at & 3))

    def cols(q):
        return pl.ds(pl.multiple_of(q * quarter, quarter), quarter)

    def unpack(q, _):
        pick = jnp.where(fits & (((b >> 2) & 3) == q), 1.0, 0.0).astype(BF16)
        for src, dst, base in ((got_f, left, 0), (got_x, left, rows), (got_g, left_g, 0)):
            dst[base:base + ROWS, cols(q)] = src[:, cols(q)]
            dst[base + ROWS:base + rows, cols(q)] = jnp.dot(
                pick, src[:, 4 * quarter:], preferred_element_type=F32).astype(BF16)
        return 0

    lax.fori_loop(0, 4, unpack, 0)
    pre[...] = jnp.zeros_like(pre)
    back[...] = jnp.zeros_like(back)

    def first(q, _):
        piece = left[:, cols(q)]
        for i, w in enumerate((gate, gate2, up, up2)):
            pre[:, i * half:(i + 1) * half] += jnp.dot(piece, w[cols(q), :], preferred_element_type=F32)
        piece_g = left_g[:, cols(q)]
        for i, w in enumerate((down, down2)):
            back[:, i * half:(i + 1) * half] += dot_nt(piece_g, w[:, cols(q)])
        return 0

    lax.fori_loop(0, 4, first, 0)
    a_f = pre[:rows, :2 * half]
    hid[...] = (a_f * jax.nn.sigmoid(a_f) * pre[:rows, 2 * half:]).astype(BF16)
    a_b = pre[rows:, :2 * half]
    sig = jax.nn.sigmoid(a_b)
    bk = back[...]
    dgate[...] = (bk * pre[rows:, 2 * half:] * sig * (1.0 + a_b * (1.0 - sig))).astype(BF16)
    dup[...] = (bk * a_b * sig).astype(BF16)
    spare[...] = jnp.zeros_like(spare)

    def second(q, _):
        pack = jnp.where(fits_t & (((at >> 2) & 3) == q), 1.0, 0.0).astype(BF16)
        y = jnp.dot(hid[:, :half], down[:, cols(q)], preferred_element_type=F32)
        y = y + jnp.dot(hid[:, half:], down2[:, cols(q)], preferred_element_type=F32)
        z = dot_nt(dgate[:, :half], gate[cols(q), :])
        z = z + dot_nt(dgate[:, half:], gate2[cols(q), :])
        z = z + dot_nt(dup[:, :half], up[cols(q), :])
        z = z + dot_nt(dup[:, half:], up2[cols(q), :])
        for i, (value, dst) in enumerate(((y, out_f), (z, out_b))):
            value = value.astype(BF16)
            dst[:, cols(q)] = value[:ROWS]
            spare[i] += jnp.dot(pack, value[ROWS:], preferred_element_type=F32)
        return 0

    lax.fori_loop(0, 4, second, 0)
    out_f[:, 4 * quarter:] = spare[0].astype(BF16)
    out_b[:, 4 * quarter:] = spare[1].astype(BF16)


def experts(got_x, got_f, got_g, gate, up, down, gate2, up2, down2):
    width, half = gate.shape
    rows = ROWS + SPARE
    vm = pl.BlockSpec(memory_space=pltpu.VMEM)
    packed = jax.ShapeDtypeStruct(got_x.shape, BF16)
    return pl.pallas_call(
        expert_kernel,
        name="experts",
        out_shape=(packed, packed),
        in_specs=[vm] * 9,
        out_specs=(vm, vm),
        scratch_shapes=[
            pltpu.VMEM((2 * rows, width), BF16), pltpu.VMEM((rows, width), BF16),
            pltpu.VMEM((2 * rows, 4 * half), F32), pltpu.VMEM((rows, 2 * half), F32),
            pltpu.VMEM((rows, 2 * half), BF16), pltpu.VMEM((rows, 2 * half), BF16),
            pltpu.VMEM((rows, 2 * half), BF16), pltpu.VMEM((2, ROWS, width // 4), F32)],
        compiler_params=pltpu.CompilerParams(vmem_limit_bytes=VMEM_LIMIT),
    )(got_x, got_f, got_g, gate, up, down, gate2, up2, down2)


def collect_kernel(code, weights, part_f, part_b, out_f, out_b,
                   back_f, back_b, mine, other, from_other, summed, from_far, final,
                   send_sem, recv_sem, csend, crecv, zsend, zrecv, osend, orecv, local_sem):
    pipe, ring, x, core = place()
    sibling = device_of(pipe, ring, x, 1 - core)
    far = device_of(pipe, ring + 4, x, core)
    half = mine.shape[2]
    quarter = half // 2
    barrier = pltpu.get_barrier_semaphore()

    def greet(who):
        pl.semaphore_signal(barrier, inc=1, device_id=who, device_id_type=MESH)

    greet(sibling)
    greet(far)
    for k in range(1, BLOCKS):
        greet(target_of(k, 0))

    @pl.when(core == 1)
    def _():
        greet(target_of(0, 0))
        pl.semaphore_wait(barrier, BLOCKS + 2)

    @pl.when(core == 0)
    def _():
        pl.semaphore_wait(barrier, BLOCKS + 1)

    def copy(t, k):
        return pltpu.make_async_remote_copy(
            src_ref=(part_f, part_b)[t].at[pl.ds(16 * k, 16)],
            dst_ref=(back_f, back_b)[t].at[pl.ds(16 * k, 16)],
            send_sem=send_sem.at[t, k], recv_sem=recv_sem.at[t, k],
            device_id=source_of(k, 0), device_id_type=MESH)

    def own(t):
        return pltpu.make_async_copy(
            (part_f, part_b)[t].at[pl.ds(0, 16)], (back_f, back_b)[t].at[pl.ds(0, 16)], local_sem.at[t])

    def across(t):
        return pltpu.make_async_remote_copy(
            src_ref=other.at[t], dst_ref=from_other.at[t], send_sem=csend.at[t], recv_sem=crecv.at[t],
            device_id=sibling, device_id_type=MESH)

    def along(t):
        return pltpu.make_async_remote_copy(
            src_ref=summed.at[t], dst_ref=from_far.at[t], send_sem=zsend.at[t], recv_sem=zrecv.at[t],
            device_id=far, device_id_type=MESH)

    my_cols = pl.ds(pl.multiple_of(core * half, half), half)

    def result(t):
        return pltpu.make_async_remote_copy(
            src_ref=final.at[t], dst_ref=(out_f, out_b)[t].at[:, my_cols],
            send_sem=osend.at[t], recv_sem=orecv.at[t], device_id=sibling, device_id_type=MESH)

    def result_here(t):
        return pltpu.make_async_copy(
            final.at[t], (out_f, out_b)[t].at[:, my_cols], local_sem.at[2 + t])

    for t in range(2):
        for k in (4, 5, 2, 3, 6, 7, 1):
            copy(t, k).start()

        @pl.when(core == 0)
        def _():
            own(t).start()

        @pl.when(core == 1)
        def _():
            copy(t, 0).start()

    lane = lax.broadcasted_iota(jnp.int32, (1, ROWS), 1)
    base = expert_of_block(lane >> 4) * CODE
    near = base + (lane & 15)
    over = base + 16 + (lane & 3)
    part = (lane >> 2) & 3

    def split(value):
        high = value.astype(BF16)
        return jnp.concatenate([high, (value - high.astype(F32)).astype(BF16)], axis=0)

    for t in range(2):
        first, second = code[:, 2 * t:2 * t + 1], code[:, 2 * t + 1:2 * t + 2]
        w0, w1 = weights[:, 2 * t:2 * t + 1], weights[:, 2 * t + 1:2 * t + 2]
        pick = split(jnp.where(first == near, w0, 0.0) + jnp.where(second == near, w1, 0.0))
        extra = split(jnp.where(first == over, w0, 0.0) + jnp.where(second == over, w1, 0.0))
        rows_ref = (back_f, back_b)[t]
        for k in range(1, BLOCKS):
            copy(t, k).wait()

        @pl.when(core == 0)
        def _():
            own(t).wait()

        @pl.when(core == 1)
        def _():
            copy(t, 0).wait()

        def chunk(q):
            cols = pl.ds(pl.multiple_of(q * quarter, quarter), quarter)
            here = jnp.where(part == q, extra, jnp.zeros_like(extra))
            both = jnp.dot(pick, rows_ref[:, cols], preferred_element_type=F32)
            both = both + jnp.dot(here, rows_ref[:, 4 * quarter:], preferred_element_type=F32)
            return both[:ROWS] + both[ROWS:]

        for i in range(2):
            other[t, :, i * quarter:(i + 1) * quarter] = chunk(2 * (1 - core) + i).astype(BF16)
        across(t).start()
        for i in range(2):
            mine[t, :, i * quarter:(i + 1) * quarter] = chunk(2 * core + i)
        across(t).wait()
        summed[t] = (mine[t] + from_other[t].astype(F32)).astype(BF16)
        along(t).start()
    for t in range(2):
        along(t).wait()
        final[t] = (summed[t].astype(F32) + from_far[t].astype(F32)).astype(BF16)
        result(t).start()
        result_here(t).start()
    for t in range(2):
        result(t).wait()
        result_here(t).wait()


def collect(code, weights, part_f, part_b, tokens, width):
    vm = pl.BlockSpec(memory_space=pltpu.VMEM)
    hbm = pl.BlockSpec(memory_space=pl.ANY)
    shape = jax.ShapeDtypeStruct((tokens, width), BF16)
    half = (2, tokens, width // 2)
    dma = pltpu.SemaphoreType.DMA
    return pl.pallas_call(
        collect_kernel,
        name="collect",
        out_shape=(shape, shape),
        in_specs=[vm, vm, hbm, hbm],
        out_specs=(hbm, hbm),
        scratch_shapes=[
            pltpu.VMEM(part_f.shape, BF16), pltpu.VMEM(part_f.shape, BF16),
            pltpu.VMEM(half, F32)] + [pltpu.VMEM(half, BF16)] * 5 + [
            dma((2, BLOCKS)), dma((2, BLOCKS)), dma((2,)), dma((2,)), dma((2,)), dma((2,)),
            dma((2,)), dma((2,)), dma((4,))],
        compiler_params=pltpu.CompilerParams(
            collective_id=1, has_side_effects=True, vmem_limit_bytes=VMEM_LIMIT),
    )(code, weights, part_f, part_b)


def slot_codes(routes):
    flat = routes.transpose(0, 2, 1).reshape(routes.shape[0], -1)
    count = flat.shape[1]
    order = jnp.arange(count, dtype=jnp.int32)
    same = (flat[:, :, None] == flat[:, None, :]) & (order[None, :] < order[:, None])[None]
    ranks = jnp.sum(same.astype(jnp.int32), axis=2)
    return (flat * CODE + ranks).reshape(routes.shape[0], routes.shape[2], routes.shape[1])


def body(fwd_in, fwd_routes, fwd_weights, bwd_saved, bwd_grad, bwd_routes, bwd_weights,
         expert_gate, expert_up, expert_down):
    tokens, width = fwd_in.shape[1:]
    codes = slot_codes(jnp.concatenate([fwd_routes, bwd_routes], axis=0))
    code_f = lax.ppermute(codes[0], "pipe", [(i, (i + 3) % 4) for i in range(4)])
    code_g = lax.ppermute(codes[1], "pipe", [(i, (i + 1) % 4) for i in range(4)])
    gate, up, down = expert_gate[0, 0], expert_up[0, 0], expert_down[0, 0]
    got_x, got_f, got_g, gate2, up2, down2 = dispatch(
        codes[1], code_f, code_g, bwd_saved[0], fwd_in[0], bwd_grad[0], gate, up, down)
    part_f, part_b = experts(got_x, got_f, got_g, gate, up, down, gate2, up2, down2)
    code_cols = codes.reshape(4, tokens).T
    weights = jnp.concatenate([fwd_weights[0], bwd_weights[0]], axis=1)
    out_f, out_b = collect(code_cols, weights, part_f, part_b, tokens, width)
    return out_f[None], out_b[None]


def solution(mesh):
    rows = P("pipe", "expert", None)
    wide = P("pipe", "expert", None, "dp")
    return jax.shard_map(
        body,
        mesh=mesh,
        in_specs=(rows,) * 7 + (wide, wide, P("pipe", "expert", "dp", None)),
        out_specs=(rows, rows),
        check_vma=False,
    )
```

time: 596 us -> 185 us (0.31)
  the two profiles are of different devices: /device:TPU:64 before, /device:TPU:201 now
where the time goes in v1:
time: 185 us
  Pallas kernels  175 us (95%)
  local copies, waits for them, and re-layouts  5.24 us (3%)
  other arithmetic  2.39 us (1%)
    pallas_call x1, Pallas kernels, collect(): pl.pallas_call(collect_kernel, name='collect', out_shape=(shape, shape),...  101 us
    pallas_call x1, Pallas kernels, dispatch(): pl.pallas_call(dispatch_kernel, name='dispatch', out_shape=(packed,) * 3...  56.8 us
    pallas_call x1, Pallas kernels, experts(): pl.pallas_call(expert_kernel, name='experts', out_shape=(packed, packed),...  16.9 us
    unnamed x11, local copies, waits for them, and re-layouts  3.73 us
  transfers between devices with their start and end apart: 2, of which 0 were waited for; matrix products, arithmetic and copies ran while one was open for 2% of the time, Pallas kernels for 0%

profile of v1, /device:TPU:201, one launch (start us, length us, event | category | flops | bytes accessed | tf_op | source)
XLA Modules:
  0.0 184.5 jit_solution(1593011250201631251)
XLA Ops:
  0.7 0.7 fusion
  1.4 0.2 convert_reduce_fusion
  1.6 0.0 copy-start.1
  1.6 1.4 collective-permute-start.1
  3.0 0.2 collective-permute-start
  3.2 0.7 bitcast_multiply_fusion
  3.9 0.7 pad_maximum_fusion
  4.6 0.7 copy.25
  5.4 0.7 copy.26.weights
  6.1 0.0 collective-permute-done.1.code_g
  6.1 0.0 copy-start.2
  6.1 0.0 collective-permute-done.code_f
  6.1 0.0 copy-start.3
  6.1 0.0 copy-done.1
  6.1 0.5 copy-done.2
  6.7 0.0 copy-done.3
  6.7 56.8 %dispatch.1 = (bf16[128,4480]{1,0:T(8,128)(2,1)}, bf16[128,4480]{1,0:T(8,128)(2,1)}, bf16[128,4480]{1,0:T(8,128)(2,1)}, bf16[3584,256]{1,0:T(8,128)(2,1)}, bf16[...) custom-call(s32[2,128]{1,0:T(2,128)} %bitcast.38, s32[2,128]{1,0:T(2,128)} %copy-done.3, s32[2,128]{1,0:T(2,128)} %copy-done.2, ...), custom_call_target="tpu_custom_call" | custom-call | tf_op jit(solution)/shard_map/dispatch/pallas_call | solution.py:157
  63.5 16.9 %experts.1 = (bf16[128,4480]{1,0:T(8,128)(2,1)}, bf16[128,4480]{1,0:T(8,128)(2,1)}) custom-call(bf16[128,4480]{1,0:T(8,128)(2,1)} %get-tuple-element.12.got_x, bf16[128,4480]{1,0:T(8,128)(2,1)} %get-tuple-element.13.got_f, bf16[128,4480]{1,0:T(8,128)(2,1)} %get-tuple-element.14.got_g, bf16[3584,256]{1,0:T(8,128)(2,1)} %bitcast.24, ...), custom_call_target="tpu_custom_call" | custom-call | tf_op jit(solution)/shard_map/experts/pallas_call | solution.py:246
  80.4 101.0 %collect.1 = (bf16[128,3584]{1,0:T(8,128)(2,1)}, bf16[128,3584]{1,0:T(8,128)(2,1)}) custom-call(s32[128,4]{1,0:T(8,128)} %bitcast.34, f32[128,4]{1,0:T(8,128)} %copy.26.weights, bf16[128,4480]{1,0:T(8,128)(2,1)} %get-tuple-element.18.part_f, bf16[128,4480]{1,0:T(8,128)(2,1)} %get-tuple-element.19.part_b), custom_call_target="tpu_custom_call" | custom-call | tf_op jit(solution)/shard_map/collect/pallas_call | solution.py:390
  181.3 0.0 copy-start
  181.3 2.2 %copy.34 = bf16[1,128,3584]{2,1,0:T(8,128)(2,1)} copy(bf16[1,128,3584]{2,1,0:T(8,128)(2,1)} %bitcast.33) | data formatting | bytes 1835008
  183.6 0.0 copy-done
  183.6 0.9 copy.35
  (6 shorter events, 0.1 us)
Async XLA Ops:
  1.6 4.5 %copy-start.1 = (s32[1,256]{1,0:T(1,128)}, s32[1,256]{1,0:T(1,128)S(1)}, u32[]{:S(2)}) copy-start(s32[1,256]{1,0:T(1,128)S(1)} %get-tuple-element.23) | copy-start | bytes 3076
  1.6 4.5 %collective-permute-start.1 = (s32[2,128]{1,0:T(2,128)S(1)}, s32[2,128]{1,0:T(2,128)S(1)}, u32[]{:S(2)}, u32[]{:S(2)}) collective-permute-start(s32[2,128]{1,0:T(2,128)S(1)} %bitcast.37), channel_id=1, source_target_pairs={{0,64},{64,128},{128,192},{192,0},{1,65},{65,129},{129,193},{193,1... | collective-permute-start | bytes 3080 | tf_op jit(solution)/shard_map/ppermute | solution.py:420
  3.0 3.1 %collective-permute-start = (s32[2,128]{1,0:T(2,128)S(1)}, s32[2,128]{1,0:T(2,128)S(1)}, u32[]{:S(2)}, u32[]{:S(2)}) collective-permute-start(s32[2,128]{1,0:T(2,128)S(1)} %bitcast.41), channel_id=1, source_target_pairs={{0,192},{64,0},{128,64},{192,128},{1,193},{65,1},{129,65},{193,129... | collective-permute-start | bytes 3080 | tf_op jit(solution)/shard_map/ppermute | solution.py:419
  6.1 0.6 copy-start.2
  6.1 0.6 copy-start.3
  181.3 2.3 %copy-start = (bf16[128,3584]{1,0:T(8,128)(2,1)S(1)}, bf16[128,3584]{1,0:T(8,128)(2,1)}, u32[]{:S(2)}) copy-start(bf16[128,3584]{1,0:T(8,128)(2,1)} %get-tuple-element.21) | copy-start | bytes 2752516

commit v2 on v0

v2 whole, which is shorter than its diff:
```python
import jax
import jax.numpy as jnp
from jax import lax
from jax.experimental import pallas as pl
from jax.experimental.pallas import tpu as pltpu
from jax.sharding import PartitionSpec as P

MESH = pl.DeviceIdType.MESH
BF16 = jnp.bfloat16
F32 = jnp.float32

BLOCKS = 8
STEP_Z = (0, 0, 1, 1, 2, -2, -1, -1)
FAR_FIRST = (4, 5, 2, 3, 6, 7, 1, 0)
CODE = 32
ROWS = BLOCKS * 16
SPARE = BLOCKS * 4
ALL = ROWS + SPARE
VMEM_LIMIT = 56 * 1024 * 1024
SECTION = (0, -1, 1)
B, F = 0, 1


def place():
    pipe = lax.axis_index("pipe")
    expert = lax.axis_index("expert")
    dp = lax.axis_index("dp")
    return pipe, (dp // 2) * 4 + expert // 4, expert % 4, dp % 2


def step_x(k, core):
    return 2 * (k % 2) + (k // 2 + core) % 2


def device_of(pipe, ring, x, core):
    ring = (ring + 16) % 8
    x = (x + 8) % 4
    return ((pipe + 4) % 4, (ring % 4) * 4 + x, (ring // 4) * 2 + core)


def target_of(k, section):
    pipe, ring, x, core = place()
    return device_of(pipe + section, ring + STEP_Z[k], x + step_x(k, core), core)


def source_of(k, section):
    pipe, ring, x, core = place()
    return device_of(pipe + section, ring - STEP_Z[k], x - step_x(k, core), core)


def expert_of_block(b):
    _, ring, x, core = place()
    away = b >> 1
    return (((ring + away) & 3) << 2) + ((x + ((b & 1) << 1) + ((away + core) & 1)) & 3)


def dot(a, b):
    return jnp.dot(a, b, preferred_element_type=F32)


def dot_nt(a, b):
    return lax.dot_general(a, b, (((1,), (1,)), ((), ())), preferred_element_type=F32)


def iota(shape, dim):
    return lax.broadcasted_iota(jnp.int32, shape, dim)


def kernel(routes_f, routes_b, weights_f, weights_b, x_ref, g_ref, f_ref, gate, up, down,
           out_f, out_b,
           send, got, left, tall, tall_down, pre, back, hid, dgate, dup, spare,
           part, home, mine, other, from_other, summed, from_far, final, codes,
           send_sem, recv_sem, wlocal, wsend, wrecv, codesend, coderecv,
           rsend, rrecv, csend, crecv, zsend, zrecv, osend, orecv, local_sem):
    pipe, ring, x, core = place()
    sibling = device_of(pipe, ring, x, 1 - core)
    far = device_of(pipe, ring + 4, x, core)
    after = device_of(pipe + 1, ring, x, core)
    before = device_of(pipe - 1, ring, x, core)
    tokens, width = x_ref.shape
    quarter = width // 4
    half = width // 2
    hidden = gate.shape[1]
    barrier = pltpu.get_barrier_semaphore()

    def greet(who):
        pl.semaphore_signal(barrier, inc=1, device_id=who, device_id_type=MESH)

    def unless_self(k, does, instead=None):
        if k:
            does()
            return
        pl.when(core == 1)(does)
        if instead is not None:
            pl.when(core == 0)(instead)

    for who in (sibling, far, after, before):
        greet(who)
    for k in range(BLOCKS):
        unless_self(k, lambda: greet(source_of(k, 0)))
        unless_self(k, lambda: greet(target_of(k, 0)))
        greet(source_of(k, -SECTION[1]))
        greet(source_of(k, -SECTION[2]))

    def here(i):
        src = (gate, up, down)[i]
        dst = tall_down.at[core] if i == 2 else tall.at[core, i]
        return pltpu.make_async_copy(src, dst, wlocal.at[i])

    def weight(i):
        src = (gate, up, down)[i]
        dst = tall_down.at[core] if i == 2 else tall.at[core, i]
        return pltpu.make_async_remote_copy(
            src_ref=src, dst_ref=dst, send_sem=wsend.at[i], recv_sem=wrecv.at[i],
            device_id=sibling, device_id_type=MESH)

    for i in range(3):
        here(i).start()

    sub, lane = iota((tokens, tokens), 0), iota((tokens, tokens), 1)

    def as_row(col):
        return jnp.sum(jnp.where(sub == lane, col, 0.0), axis=0, keepdims=True)

    def as_col(row):
        return jnp.sum(jnp.where(sub == lane, row, 0.0), axis=1, keepdims=True)

    def count(flags):
        return jnp.sum(jnp.where(flags, 1.0, 0.0), axis=0, keepdims=True)

    def code_rows(routes):
        c0, c1 = routes[:, 0:1].astype(F32), routes[:, 1:2].astype(F32)
        r0, r1 = as_row(c0), as_row(c1)
        rank0 = count((c0 == r0) & (sub < lane))
        rank1 = count(c0 == r1) + count((c1 == r1) & (sub < lane))
        return r0 * CODE + rank0, r1 * CODE + rank1

    cols = []
    codes[0:2] = jnp.zeros_like(codes[0:2])
    for i, routes in enumerate((routes_b, routes_f)):
        first, second = code_rows(routes)
        codes[i, 0:1, :] = first
        codes[i, 1:2, :] = second
        cols.append((as_col(first), as_col(second)))

    def swap(i):
        return pltpu.make_async_remote_copy(
            src_ref=codes.at[i], dst_ref=codes.at[2 + i], send_sem=codesend.at[i], recv_sem=coderecv.at[i],
            device_id=(after, before)[i], device_id_type=MESH)

    def blocks_of(index):
        expert = expert_of_block(index >> 4) * CODE
        return (expert + (index & 15)).astype(F32), (expert + 16 + (index & 3)).astype(F32), (index >> 2) & 3

    near_col, over_col, part_col = blocks_of(iota((ROWS, 1), 0))

    def build(t, code, rows_ref):
        first, second = codes[code, 0:1, :], codes[code, 1:2, :]
        pick = jnp.where((first == near_col) | (second == near_col), 1.0, 0.0).astype(BF16)
        extra = jnp.where((first == over_col) | (second == over_col), 1.0, 0.0)
        total = jnp.zeros((ROWS, quarter), F32)
        for q in range(4):
            piece = rows_ref[:, q * quarter:(q + 1) * quarter]
            send[t, :, q * quarter:(q + 1) * quarter] = dot(pick, piece).astype(BF16)
            total = total + dot(jnp.where(part_col == q, extra, 0.0).astype(BF16), piece)
        send[t, :, width:] = total.astype(BF16)

    def outward(t, k):
        block = pl.ds(16 * k, 16)
        return pltpu.make_async_remote_copy(
            src_ref=send.at[t, block], dst_ref=got.at[t, block],
            send_sem=send_sem.at[t, k], recv_sem=recv_sem.at[t, k],
            device_id=target_of(k, SECTION[t]), device_id_type=MESH)

    def own_outward():
        return pltpu.make_async_copy(send.at[0, pl.ds(0, 16)], got.at[0, pl.ds(0, 16)], local_sem.at[0])

    def send_out(t):
        for k in FAR_FIRST:
            if t == 0:
                unless_self(k, lambda: outward(t, k).start(), lambda: own_outward().start())
            else:
                outward(t, k).start()

    def wait_out(t):
        for k in FAR_FIRST:
            if t == 0:
                unless_self(k, lambda: outward(t, k).wait(), lambda: own_outward().wait())
            else:
                outward(t, k).wait()

    build(0, 0, x_ref)
    pl.semaphore_wait(barrier, 4 * BLOCKS + 2 + 2 * core)
    swap(0).start()
    swap(1).start()
    send_out(0)
    for i in range(3):
        weight(i).start()
    swap(0).wait()
    build(1, 2, g_ref)
    send_out(1)
    swap(1).wait()
    build(2, 3, f_ref)
    send_out(2)

    a, b = iota((SPARE, ROWS), 0), iota((SPARE, ROWS), 1)
    fits = ((a >> 2) == (b >> 4)) & ((a & 3) == (b & 3))
    at, bt = iota((ROWS, SPARE), 0), iota((ROWS, SPARE), 1)
    fits_t = ((bt >> 2) == (at >> 4)) & ((bt & 3) == (at & 3))

    def columns(q):
        return pl.ds(pl.multiple_of(q * quarter, quarter), quarter)

    def unpack(t):
        def step(q, _):
            pick = jnp.where(fits & (((b >> 2) & 3) == q), 1.0, 0.0).astype(BF16)
            left[:ROWS, columns(q)] = got[t, :, columns(q)]
            left[ROWS:, columns(q)] = dot(pick, got[t, :, width:]).astype(BF16)
            return 0
        lax.fori_loop(0, 4, step, 0)

    def first_layer():
        pre[...] = jnp.zeros_like(pre)

        def step(q, _):
            piece = left[:, columns(q)]
            for c in range(2):
                for i in range(2):
                    lo = (2 * i + c) * hidden
                    pre[:, lo:lo + hidden] += dot(piece, tall[c, i, columns(q), :])
            return 0
        lax.fori_loop(0, 4, step, 0)

    def back_layer():
        back[...] = jnp.zeros_like(back)

        def step(q, _):
            piece = left[:, columns(q)]
            for c in range(2):
                back[:, c * hidden:(c + 1) * hidden] += dot_nt(piece, tall_down[c, :, columns(q)])
            return 0
        lax.fori_loop(0, 4, step, 0)

    def second_layer(r, product):
        spare[...] = jnp.zeros_like(spare)

        def step(q, _):
            pack = jnp.where(fits_t & (((at >> 2) & 3) == q), 1.0, 0.0).astype(BF16)
            value = product(q).astype(BF16)
            part[r, :, columns(q)] = value[:ROWS]
            spare[...] += dot(pack, value[ROWS:])
            return 0
        lax.fori_loop(0, 4, step, 0)
        part[r, :, width:] = spare[...].astype(BF16)

    def forward_product(q):
        return (dot(hid[:, :hidden], tall_down[0, :, columns(q)])
                + dot(hid[:, hidden:], tall_down[1, :, columns(q)]))

    def backward_product(q):
        total = dot_nt(dgate[:, :hidden], tall[0, 0, columns(q), :])
        total = total + dot_nt(dgate[:, hidden:], tall[1, 0, columns(q), :])
        total = total + dot_nt(dup[:, :hidden], tall[0, 1, columns(q), :])
        return total + dot_nt(dup[:, hidden:], tall[1, 1, columns(q), :])

    def homeward(r, k):
        block = pl.ds(16 * k, 16)
        return pltpu.make_async_remote_copy(
            src_ref=part.at[r, block], dst_ref=home.at[r, block],
            send_sem=rsend.at[r, k], recv_sem=rrecv.at[r, k],
            device_id=source_of(k, 0), device_id_type=MESH)

    def own_homeward(r):
        return pltpu.make_async_copy(part.at[r, pl.ds(0, 16)], home.at[r, pl.ds(0, 16)], local_sem.at[1 + r])

    def send_home(r):
        for k in FAR_FIRST:
            unless_self(k, lambda: homeward(r, k).start(), lambda: own_homeward(r).start())

    def wait_home(r):
        for k in FAR_FIRST:
            unless_self(k, lambda: homeward(r, k).wait(), lambda: own_homeward(r).wait())

    for i in range(3):
        here(i).wait()
        weight(i).wait()
    wait_out(0)
    unpack(0)
    first_layer()
    wait_out(1)
    unpack(1)
    back_layer()
    pre_a = pre[:, :2 * hidden]
    sig = jax.nn.sigmoid(pre_a)
    bk = back[...]
    dgate[...] = (bk * pre[:, 2 * hidden:] * sig * (1.0 + pre_a * (1.0 - sig))).astype(BF16)
    dup[...] = (bk * pre_a * sig).astype(BF16)
    second_layer(B, backward_product)
    send_home(B)
    wait_out(2)
    unpack(2)
    first_layer()
    pre_a = pre[:, :2 * hidden]
    hid[...] = (pre_a * jax.nn.sigmoid(pre_a) * pre[:, 2 * hidden:]).astype(BF16)
    second_layer(F, forward_product)
    send_home(F)

    near_row, over_row, part_row = blocks_of(iota((1, ROWS), 1))
    my_cols = pl.ds(pl.multiple_of(core * half, half), half)

    def split(value):
        high = value.astype(BF16)
        return jnp.concatenate([high, (value - high.astype(F32)).astype(BF16)], axis=0)

    def across(r):
        return pltpu.make_async_remote_copy(
            src_ref=other.at[r], dst_ref=from_other.at[r], send_sem=csend.at[r], recv_sem=crecv.at[r],
            device_id=sibling, device_id_type=MESH)

    def along(r):
        return pltpu.make_async_remote_copy(
            src_ref=summed.at[r], dst_ref=from_far.at[r], send_sem=zsend.at[r], recv_sem=zrecv.at[r],
            device_id=far, device_id_type=MESH)

    def result(r):
        return pltpu.make_async_remote_copy(
            src_ref=final.at[r], dst_ref=(out_b, out_f)[r].at[:, my_cols],
            send_sem=osend.at[r], recv_sem=orecv.at[r], device_id=sibling, device_id_type=MESH)

    def result_here(r):
        return pltpu.make_async_copy(final.at[r], (out_b, out_f)[r].at[:, my_cols], local_sem.at[3 + r])

    for r in (B, F):
        weights = (weights_b, weights_f)[r]
        w0, w1 = weights[:, 0:1], weights[:, 1:2]
        first, second = cols[r]
        pick = split(jnp.where(first == near_row, w0, 0.0) + jnp.where(second == near_row, w1, 0.0))
        extra = split(jnp.where(first == over_row, w0, 0.0) + jnp.where(second == over_row, w1, 0.0))
        wait_home(r)

        def chunk(q):
            mask = jnp.where(part_row == q, extra, jnp.zeros_like(extra))
            both = dot(pick, home[r, :, columns(q)]) + dot(mask, home[r, :, width:])
            return both[:tokens] + both[tokens:]

        for i in range(2):
            other[r, :, i * quarter:(i + 1) * quarter] = chunk(2 * (1 - core) + i).astype(BF16)
        across(r).start()
        for i in range(2):
            mine[:, i * quarter:(i + 1) * quarter] = chunk(2 * core + i)
        across(r).wait()
        summed[r] = (mine[...] + from_other[r].astype(F32)).astype(BF16)
        along(r).start()
    for r in (B, F):
        along(r).wait()
        final[r] = (summed[r].astype(F32) + from_far[r].astype(F32)).astype(BF16)
        result(r).start()
        result_here(r).start()
    for r in (B, F):
        result(r).wait()
        result_here(r).wait()


def body(fwd_in, fwd_routes, fwd_weights, bwd_saved, bwd_grad, bwd_routes, bwd_weights,
         expert_gate, expert_up, expert_down):
    tokens, width = fwd_in.shape[1:]
    hidden = expert_gate.shape[3]
    packed = (ROWS, width + width // 4)
    half = (2, tokens, width // 2)
    vm = pl.BlockSpec(memory_space=pltpu.VMEM)
    hbm = pl.BlockSpec(memory_space=pl.ANY)
    dma = pltpu.SemaphoreType.DMA
    shape = jax.ShapeDtypeStruct((tokens, width), BF16)
    out_f, out_b = pl.pallas_call(
        kernel,
        name="experts",
        out_shape=(shape, shape),
        in_specs=[vm] * 7 + [hbm] * 3,
        out_specs=(hbm, hbm),
        scratch_shapes=[
            pltpu.VMEM((3,) + packed, BF16), pltpu.VMEM((3,) + packed, BF16),
            pltpu.VMEM((ALL, width), BF16),
            pltpu.VMEM((2, 2, width, hidden), BF16), pltpu.VMEM((2, hidden, width), BF16),
            pltpu.VMEM((ALL, 4 * hidden), F32), pltpu.VMEM((ALL, 2 * hidden), F32),
            pltpu.VMEM((ALL, 2 * hidden), BF16), pltpu.VMEM((ALL, 2 * hidden), BF16),
            pltpu.VMEM((ALL, 2 * hidden), BF16),
            pltpu.VMEM((ROWS, width // 4), F32),
            pltpu.VMEM((2,) + packed, BF16), pltpu.VMEM((2,) + packed, BF16),
            pltpu.VMEM(half[1:], F32)] + [pltpu.VMEM(half, BF16)] * 5 + [
            pltpu.VMEM((4, 8, 128), F32),
            dma((3, BLOCKS)), dma((3, BLOCKS)), dma((3,)), dma((3,)), dma((3,)), dma((2,)), dma((2,)),
            dma((2, BLOCKS)), dma((2, BLOCKS)), dma((2,)), dma((2,)), dma((2,)), dma((2,)),
            dma((2,)), dma((2,)), dma((5,))],
        compiler_params=pltpu.CompilerParams(
            collective_id=0, has_side_effects=True, vmem_limit_bytes=VMEM_LIMIT),
    )(fwd_routes[0], bwd_routes[0], fwd_weights[0], bwd_weights[0], bwd_saved[0], bwd_grad[0], fwd_in[0],
      expert_gate[0, 0], expert_up[0, 0], expert_down[0, 0])
    return out_f[None], out_b[None]


def solution(mesh):
    rows = P("pipe", "expert", None)
    wide = P("pipe", "expert", None, "dp")
    return jax.shard_map(
        body,
        mesh=mesh,
        in_specs=(rows,) * 7 + (wide, wide, P("pipe", "expert", "dp", None)),
        out_specs=(rows, rows),
        check_vma=False,
    )
```

time: 596 us -> 159 us (0.27)
  the two profiles are of different devices: /device:TPU:64 before, /device:TPU:109 now
where the time goes in v2:
time: 159 us
  Pallas kernels  150 us (94%)
  local copies, waits for them, and re-layouts  8.79 us (6%)
    pallas_call x1, Pallas kernels, body(): pl.pallas_call(kernel, name='experts', out_shape=(shape, shape), in_specs...  150 us
    unnamed x8, local copies, waits for them, and re-layouts  8.79 us

profile of v2, /device:TPU:109, one launch (start us, length us, event | category | flops | bytes accessed | tf_op | source)
XLA Modules:
  0.0 159.1 jit_solution(14043262342754349921)
XLA Ops:
  0.6 1.4 copy.12
  2.0 1.4 copy.14
  3.4 1.4 copy.13
  4.9 1.4 copy.15
  6.3 149.7 %experts.1 = (bf16[128,3584]{1,0:T(8,128)(2,1)}, bf16[128,3584]{1,0:T(8,128)(2,1)}) custom-call(s32[128,2]{1,0:T(8,128)} %bitcast.20, s32[128,2]{1,0:T(8,128)} %bitcast.22, f32[128,2]{1,0:T(8,128)} %bitcast.21, f32[128,2]{1,0:T(8,128)} %bitcast.23, bf16[128,3584]{1,0:T(8,128)(2,1)} %bitcast.15, bf16[128,3584]{1,0:T(8,128)(2,1)} %bitcast.16, ...), custom_call_target="tpu_custom_call" | custom-call | tf_op jit(solution)/shard_map/experts/pallas_call | solution.py:374
  155.9 0.0 copy-start
  155.9 2.2 %copy.18 = bf16[1,128,3584]{2,1,0:T(8,128)(2,1)} copy(bf16[1,128,3584]{2,1,0:T(8,128)(2,1)} %bitcast.19) | data formatting | bytes 1835008
  158.2 0.0 copy-done
  158.2 0.9 copy.19
Async XLA Ops:
  155.9 2.3 %copy-start = (bf16[128,3584]{1,0:T(8,128)(2,1)S(1)}, bf16[128,3584]{1,0:T(8,128)(2,1)}, u32[]{:S(2)}) copy-start(bf16[128,3584]{1,0:T(8,128)(2,1)} %get-tuple-element.5) | copy-start | bytes 2752516

commit v3 on v2

v3 whole, which is shorter than its diff:
```python
import jax
import jax.numpy as jnp
from jax import lax
from jax.experimental import pallas as pl
from jax.experimental.pallas import tpu as pltpu
from jax.sharding import PartitionSpec as P

MESH = pl.DeviceIdType.MESH
BF16 = jnp.bfloat16
F32 = jnp.float32

BLOCKS = 8
STEP_Z = (0, 0, 1, 1, 2, -2, -1, -1)
FAR_FIRST = (4, 5, 2, 3, 6, 7, 1, 0)
CODE = 32
ROWS = BLOCKS * 16
SPARE = BLOCKS * 4
ALL = ROWS + SPARE
VMEM_LIMIT = 56 * 1024 * 1024
SECTION = (0, -1, 1)
GROUP = 512
FOLD = GROUP // 4
WIDE = GROUP + FOLD
CHUNKS = 2
B, F = 0, 1


def place():
    pipe = lax.axis_index("pipe")
    expert = lax.axis_index("expert")
    dp = lax.axis_index("dp")
    return pipe, (dp // 2) * 4 + expert // 4, expert % 4, dp % 2


def step_x(k, core):
    return 2 * (k % 2) + (k // 2 + core) % 2


def device_of(pipe, ring, x, core):
    ring = (ring + 16) % 8
    x = (x + 8) % 4
    return ((pipe + 4) % 4, (ring % 4) * 4 + x, (ring // 4) * 2 + core)


def target_of(k):
    pipe, ring, x, core = place()
    return device_of(pipe, ring + STEP_Z[k], x + step_x(k, core), core)


def source_of(k):
    pipe, ring, x, core = place()
    return device_of(pipe, ring - STEP_Z[k], x - step_x(k, core), core)


def expert_of_block(b):
    _, ring, x, core = place()
    away = b >> 1
    return (((ring + away) & 3) << 2) + ((x + ((b & 1) << 1) + ((away + core) & 1)) & 3)


def dot(a, b):
    return jnp.dot(a, b, preferred_element_type=F32)


def dot_nt(a, b):
    return lax.dot_general(a, b, (((1,), (1,)), ((), ())), preferred_element_type=F32)


def iota(shape, dim):
    return lax.broadcasted_iota(jnp.int32, shape, dim)


def kernel(routes_f, routes_b, weights_f, weights_b, x_ref, g_ref, f_ref, gate, up, down,
           out_f, out_b,
           send, got, left, tall, tall_down, pre, back, hid, dgate, dup,
           part, home, comb, mine, other, from_other, summed, from_far, final, moved,
           send_sem, recv_sem, wlocal, wsend, wrecv, shift_send, shift_recv, pass_send, pass_recv,
           rsend, rrecv, rlocal, csend, crecv, zsend, zrecv, osend, orecv, olocal, local_sem):
    pipe, ring, x, core = place()
    sibling = device_of(pipe, ring, x, 1 - core)
    far = device_of(pipe, ring + 4, x, core)
    after = device_of(pipe + 1, ring, x, core)
    before = device_of(pipe - 1, ring, x, core)
    tokens, width = x_ref.shape
    quarter = width // 4
    groups = width // GROUP
    cuts = [groups * i // CHUNKS for i in range(CHUNKS + 1)]
    hidden = gate.shape[1]
    barrier = pltpu.get_barrier_semaphore()

    def greet(who):
        pl.semaphore_signal(barrier, inc=1, device_id=who, device_id_type=MESH)

    def unless_self(k, does, instead=None):
        if k:
            does()
            return
        pl.when(core == 1)(does)
        if instead is not None:
            pl.when(core == 0)(instead)

    for who in (sibling, far, after, before):
        greet(who)
    for k in range(BLOCKS):
        unless_self(k, lambda: greet(source_of(k)))
        unless_self(k, lambda: greet(target_of(k)))

    def here(i):
        src = (gate, up, down)[i]
        dst = tall_down.at[core] if i == 2 else tall.at[core, i]
        return pltpu.make_async_copy(src, dst, wlocal.at[i])

    def weight(i):
        src = (gate, up, down)[i]
        dst = tall_down.at[core] if i == 2 else tall.at[core, i]
        return pltpu.make_async_remote_copy(
            src_ref=src, dst_ref=dst, send_sem=wsend.at[i], recv_sem=wrecv.at[i],
            device_id=sibling, device_id_type=MESH)

    for i in range(3):
        here(i).start()

    sub, lane = iota((tokens, tokens), 0), iota((tokens, tokens), 1)

    def as_col(row):
        return jnp.sum(jnp.where(sub == lane, row, 0.0), axis=1, keepdims=True)

    def count(flags):
        return jnp.sum(jnp.where(flags, 1.0, 0.0), axis=0, keepdims=True)

    def code_rows(routes):
        r0, r1 = routes[0:1, :].astype(F32), routes[1:2, :].astype(F32)
        c0, c1 = as_col(r0), as_col(r1)
        rank0 = count((c0 == r0) & (sub < lane))
        rank1 = count(c0 == r1) + count((c1 == r1) & (sub < lane))
        return r0 * CODE + rank0, r1 * CODE + rank1

    half = tokens // 2
    my_half = pl.ds(pl.multiple_of(core * half, half), half)

    def shift(t):
        return pltpu.make_async_remote_copy(
            src_ref=(None, g_ref, f_ref)[t].at[my_half], dst_ref=moved.at[t - 1, my_half],
            send_sem=shift_send.at[t - 1], recv_sem=shift_recv.at[t - 1],
            device_id=(None, before, after)[t], device_id_type=MESH)

    def pass_on(t):
        return pltpu.make_async_remote_copy(
            src_ref=moved.at[t - 1, my_half], dst_ref=moved.at[t - 1, my_half],
            send_sem=pass_send.at[t - 1], recv_sem=pass_recv.at[t - 1],
            device_id=sibling, device_id_type=MESH)

    def blocks_of(index):
        expert = expert_of_block(index >> 4) * CODE
        return (expert + (index & 15)).astype(F32), (expert + 16 + (index & 3)).astype(F32), (index >> 2) & 3

    near_col, over_col, part_col = blocks_of(iota((ROWS, 1), 0))

    def build(t, code, rows_ref):
        first, second = code
        pick = jnp.where((first == near_col) | (second == near_col), 1.0, 0.0).astype(BF16)
        extra = jnp.where((first == over_col) | (second == over_col), 1.0, 0.0)
        total = jnp.zeros((ROWS, quarter), F32)
        for q in range(4):
            piece = rows_ref[:, q * quarter:(q + 1) * quarter]
            send[t, :, q * quarter:(q + 1) * quarter] = dot(pick, piece).astype(BF16)
            total = total + dot(jnp.where(part_col == q, extra, 0.0).astype(BF16), piece)
        send[t, :, width:] = total.astype(BF16)

    def outward(t, k):
        block = pl.ds(16 * k, 16)
        return pltpu.make_async_remote_copy(
            src_ref=send.at[t, block], dst_ref=got.at[t, block],
            send_sem=send_sem.at[t, k], recv_sem=recv_sem.at[t, k],
            device_id=target_of(k), device_id_type=MESH)

    def own_outward(t):
        return pltpu.make_async_copy(send.at[t, pl.ds(0, 16)], got.at[t, pl.ds(0, 16)], local_sem.at[t])

    def send_out(t):
        for k in FAR_FIRST:
            unless_self(k, lambda: outward(t, k).start(), lambda: own_outward(t).start())

    def wait_out(t):
        for k in FAR_FIRST:
            unless_self(k, lambda: outward(t, k).wait(), lambda: own_outward(t).wait())

    pl.semaphore_wait(barrier, 2 * BLOCKS + 2 + 2 * core)
    shift(1).start()
    shift(2).start()
    for i in range(3):
        weight(i).start()
    codes = [code_rows(routes) for routes in (routes_b, routes_f)]
    build(0, codes[B], x_ref)
    send_out(0)
    for t in (1, 2):
        shift(t).wait()
        pass_on(t).start()
    for t in (1, 2):
        pass_on(t).wait()
        build(t, codes[t - 1], moved.at[t - 1])
        send_out(t)

    near_row, over_row, part_row = blocks_of(iota((1, ROWS), 1))
    for r, weights in enumerate((weights_b, weights_f)):
        w0, w1 = as_col(weights[0:1, :]), as_col(weights[1:2, :])
        first, second = as_col(codes[r][0]), as_col(codes[r][1])
        pick = jnp.where(first == near_row, w0, 0.0) + jnp.where(second == near_row, w1, 0.0)
        extra = jnp.where(first == over_row, w0, 0.0) + jnp.where(second == over_row, w1, 0.0)
        for j in range(5):
            value = pick if j == 0 else jnp.where(part_row == j - 1, extra, 0.0)
            high = value.astype(BF16)
            comb[r, j, :tokens, :] = high
            comb[r, j, tokens:, :] = (value - high.astype(F32)).astype(BF16)

    a, b = iota((SPARE, ROWS), 0), iota((SPARE, ROWS), 1)
    fits = ((a >> 2) == (b >> 4)) & ((a & 3) == (b & 3))
    at, bt = iota((ROWS, SPARE), 0), iota((ROWS, SPARE), 1)
    fits_t = ((bt >> 2) == (at >> 4)) & ((bt & 3) == (at & 3))

    def columns(q):
        return pl.ds(pl.multiple_of(q * quarter, quarter), quarter)

    def unpack(t):
        def step(q, _):
            pick = jnp.where(fits & (((b >> 2) & 3) == q), 1.0, 0.0).astype(BF16)
            left[:ROWS, columns(q)] = got[t, :, columns(q)]
            left[ROWS:, columns(q)] = dot(pick, got[t, :, width:]).astype(BF16)
            return 0
        lax.fori_loop(0, 4, step, 0)

    def first_layer():
        pre[...] = jnp.zeros_like(pre)

        def step(q, _):
            piece = left[:, columns(q)]
            for c in range(2):
                for i in range(2):
                    lo = (2 * i + c) * hidden
                    pre[:, lo:lo + hidden] += dot(piece, tall[c, i, columns(q), :])
            return 0
        lax.fori_loop(0, 4, step, 0)

    def back_layer():
        back[...] = jnp.zeros_like(back)

        def step(q, _):
            piece = left[:, columns(q)]
            for c in range(2):
                back[:, c * hidden:(c + 1) * hidden] += dot_nt(piece, tall_down[c, :, columns(q)])
            return 0
        lax.fori_loop(0, 4, step, 0)

    packs = [jnp.where(fits_t & (((at >> 2) & 3) == q), 1.0, 0.0).astype(BF16) for q in range(4)]

    def group_cols(g, start=0, size=GROUP, pitch=GROUP):
        return pl.ds(pl.multiple_of(g * pitch + start, FOLD), size)

    def second_layer(r, n, product):
        def step(g, _):
            value = product(group_cols(g)).astype(BF16)
            part[r, :, group_cols(g, 0, GROUP, WIDE)] = value[:ROWS]
            rest = value[ROWS:]
            folded = dot(packs[0], rest[:, :FOLD])
            for q in range(1, 4):
                folded = folded + dot(packs[q], rest[:, q * FOLD:(q + 1) * FOLD])
            part[r, :, group_cols(g, GROUP, FOLD, WIDE)] = folded.astype(BF16)
            return 0
        lax.fori_loop(cuts[n], cuts[n + 1], step, 0)

    def forward_product(span):
        return dot(hid[:, :hidden], tall_down[0, :, span]) + dot(hid[:, hidden:], tall_down[1, :, span])

    def backward_product(span):
        total = dot_nt(dgate[:, :hidden], tall[0, 0, span, :])
        total = total + dot_nt(dgate[:, hidden:], tall[1, 0, span, :])
        total = total + dot_nt(dup[:, :hidden], tall[0, 1, span, :])
        return total + dot_nt(dup[:, hidden:], tall[1, 1, span, :])

    def packed_cols(n):
        return pl.ds(cuts[n] * WIDE, (cuts[n + 1] - cuts[n]) * WIDE)

    def homeward(r, n, k):
        block = pl.ds(16 * k, 16)
        return pltpu.make_async_remote_copy(
            src_ref=part.at[r, block, packed_cols(n)], dst_ref=home.at[r, block, packed_cols(n)],
            send_sem=rsend.at[r, n, k], recv_sem=rrecv.at[r, n, k],
            device_id=source_of(k), device_id_type=MESH)

    def own_homeward(r, n):
        block = pl.ds(0, 16)
        return pltpu.make_async_copy(
            part.at[r, block, packed_cols(n)], home.at[r, block, packed_cols(n)], rlocal.at[r, n])

    def send_home(r, n):
        for k in FAR_FIRST:
            unless_self(k, lambda: homeward(r, n, k).start(), lambda: own_homeward(r, n).start())

    def wait_home(r, n):
        for k in FAR_FIRST:
            unless_self(k, lambda: homeward(r, n, k).wait(), lambda: own_homeward(r, n).wait())

    for i in range(3):
        here(i).wait()
        weight(i).wait()
    wait_out(0)
    unpack(0)
    first_layer()
    wait_out(1)
    unpack(1)
    back_layer()
    pre_a = pre[:, :2 * hidden]
    sig = jax.nn.sigmoid(pre_a)
    bk = back[...]
    dgate[...] = (bk * pre[:, 2 * hidden:] * sig * (1.0 + pre_a * (1.0 - sig))).astype(BF16)
    dup[...] = (bk * pre_a * sig).astype(BF16)
    for n in range(CHUNKS):
        second_layer(B, n, backward_product)
        send_home(B, n)
    wait_out(2)
    unpack(2)
    first_layer()
    pre_a = pre[:, :2 * hidden]
    hid[...] = (pre_a * jax.nn.sigmoid(pre_a) * pre[:, 2 * hidden:]).astype(BF16)
    for n in range(CHUNKS):
        second_layer(F, n, forward_product)
        send_home(F, n)

    def span_of(n):
        return pl.ds(cuts[n] * GROUP, (cuts[n + 1] - cuts[n]) * GROUP)

    def half_of(which):
        return pl.multiple_of(which * half, half)

    def across(r, n):
        return pltpu.make_async_remote_copy(
            src_ref=other.at[r, :, span_of(n)], dst_ref=from_other.at[r, :, span_of(n)],
            send_sem=csend.at[r, n], recv_sem=crecv.at[r, n], device_id=sibling, device_id_type=MESH)

    def along(r, n):
        return pltpu.make_async_remote_copy(
            src_ref=summed.at[r, :, span_of(n)], dst_ref=from_far.at[r, :, span_of(n)],
            send_sem=zsend.at[r, n], recv_sem=zrecv.at[r, n], device_id=far, device_id_type=MESH)

    def my_result(r, n):
        return (out_b, out_f)[r].at[pl.ds(half_of(core), half), span_of(n)]

    def result(r, n):
        return pltpu.make_async_remote_copy(
            src_ref=final.at[r, :, span_of(n)], dst_ref=my_result(r, n),
            send_sem=osend.at[r, n], recv_sem=orecv.at[r, n], device_id=sibling, device_id_type=MESH)

    def result_here(r, n):
        return pltpu.make_async_copy(final.at[r, :, span_of(n)], my_result(r, n), olocal.at[r, n])

    def combine(r, n, which, dst):
        def rows_of(j):
            start = half_of(which)
            return jnp.concatenate([comb[r, j, pl.ds(start, half), :],
                                    comb[r, j, pl.ds(tokens + start, half), :]], axis=0)
        mats = [rows_of(j) for j in range(5)]

        def step(g, _):
            folded = home[r, :, group_cols(g, GROUP, FOLD, WIDE)]
            both = dot(mats[0], home[r, :, group_cols(g, 0, GROUP, WIDE)])
            both = both + jnp.concatenate([dot(m, folded) for m in mats[1:]], axis=1)
            dst[r, :, group_cols(g)] = (both[:half] + both[half:]).astype(dst.dtype)
            return 0
        lax.fori_loop(cuts[n], cuts[n + 1], step, 0)

    def gather(r):
        for n in range(CHUNKS):
            wait_home(r, n)
            combine(r, n, 1 - core, other)
            across(r, n).start()
            combine(r, n, core, mine)
            span = span_of(n)
            across(r, n).wait()
            summed[r, :, span] = (mine[r, :, span] + from_other[r, :, span].astype(F32)).astype(BF16)
            along(r, n).start()

    def finish(r):
        for n in range(CHUNKS):
            span = span_of(n)
            along(r, n).wait()
            final[r, :, span] = (summed[r, :, span].astype(F32) + from_far[r, :, span].astype(F32)).astype(BF16)
            result(r, n).start()
            result_here(r, n).start()

    gather(B)
    gather(F)
    finish(B)
    finish(F)
    for r in (B, F):
        for n in range(CHUNKS):
            result(r, n).wait()
            result_here(r, n).wait()


def body(fwd_in, fwd_routes, fwd_weights, bwd_saved, bwd_grad, bwd_routes, bwd_weights,
         expert_gate, expert_up, expert_down):
    tokens, width = fwd_in.shape[1:]
    hidden = expert_gate.shape[3]
    packed = (ROWS, width + width // 4)
    half = (2, tokens // 2, width)
    vm = pl.BlockSpec(memory_space=pltpu.VMEM)
    hbm = pl.BlockSpec(memory_space=pl.ANY)
    dma = pltpu.SemaphoreType.DMA
    shape = jax.ShapeDtypeStruct((tokens, width), BF16)
    out_f, out_b = pl.pallas_call(
        kernel,
        name="experts",
        out_shape=(shape, shape),
        in_specs=[vm] * 5 + [hbm] * 5,
        out_specs=(hbm, hbm),
        scratch_shapes=[
            pltpu.VMEM((3,) + packed, BF16), pltpu.VMEM((3,) + packed, BF16),
            pltpu.VMEM((ALL, width), BF16),
            pltpu.VMEM((2, 2, width, hidden), BF16), pltpu.VMEM((2, hidden, width), BF16),
            pltpu.VMEM((ALL, 4 * hidden), F32), pltpu.VMEM((ALL, 2 * hidden), F32),
            pltpu.VMEM((ALL, 2 * hidden), BF16), pltpu.VMEM((ALL, 2 * hidden), BF16),
            pltpu.VMEM((ALL, 2 * hidden), BF16),
            pltpu.VMEM((2,) + packed, BF16), pltpu.VMEM((2,) + packed, BF16),
            pltpu.VMEM((2, 5, 2 * tokens, ROWS), BF16),
            pltpu.VMEM(half, F32)] + [pltpu.VMEM(half, BF16)] * 5 + [
            pltpu.VMEM((2, tokens, width), BF16),
            dma((3, BLOCKS)), dma((3, BLOCKS)), dma((3,)), dma((3,)), dma((3,)),
            dma((2,)), dma((2,)), dma((2,)), dma((2,)),
            dma((2, CHUNKS, BLOCKS)), dma((2, CHUNKS, BLOCKS)), dma((2, CHUNKS)),
            dma((2, CHUNKS)), dma((2, CHUNKS)), dma((2, CHUNKS)), dma((2, CHUNKS)),
            dma((2, CHUNKS)), dma((2, CHUNKS)), dma((2, CHUNKS)), dma((3,))],
        compiler_params=pltpu.CompilerParams(
            collective_id=0, has_side_effects=True, vmem_limit_bytes=VMEM_LIMIT),
    )(fwd_routes[0].T, bwd_routes[0].T, fwd_weights[0].T, bwd_weights[0].T, bwd_saved[0], bwd_grad[0], fwd_in[0],
      expert_gate[0, 0], expert_up[0, 0], expert_down[0, 0])
    return out_f[None], out_b[None]


def solution(mesh):
    rows = P("pipe", "expert", None)
    wide = P("pipe", "expert", None, "dp")
    return jax.shard_map(
        body,
        mesh=mesh,
        in_specs=(rows,) * 7 + (wide, wide, P("pipe", "expert", "dp", None)),
        out_specs=(rows, rows),
        check_vma=False,
    )
```

time: 159 us -> 138 us (0.87)
  the two profiles are of different devices: /device:TPU:109 before, /device:TPU:41 now
where the time goes in v3:
time: 138 us; the launch traced here: 137 us
  Pallas kernels  134 us (97%)
  local copies, waits for them, and re-layouts  3.17 us (2%)
    pallas_call x1, Pallas kernels, body(): pl.pallas_call(kernel, name='experts', out_shape=(shape, shape), in_specs...  134 us
    unnamed x4, local copies, waits for them, and re-layouts  3.17 us

profile of v3, /device:TPU:41, one launch (start us, length us, event | category | flops | bytes accessed | tf_op | source)
XLA Modules:
  0.0 137.4 jit_solution(16285826599276588197)
XLA Ops:
  0.6 133.6 %experts.1 = (bf16[128,3584]{1,0:T(8,128)(2,1)}, bf16[128,3584]{1,0:T(8,128)(2,1)}) custom-call(s32[2,128]{1,0:T(2,128)} %bitcast.28, s32[2,128]{1,0:T(2,128)} %bitcast.29, f32[2,128]{1,0:T(2,128)} %bitcast.30, f32[2,128]{1,0:T(2,128)} %bitcast.31, bf16[128,3584]{1,0:T(8,128)(2,1)} %bitcast.23, bf16[128,3584]{1,0:T(8,128)(2,1)} %bitcast.24, ...), custom_call_target="tpu_custom_call" | custom-call | tf_op jit(solution)/shard_map/experts/pallas_call | solution.py:410
  134.2 0.0 copy-start
  134.3 2.2 %copy.14 = bf16[1,128,3584]{2,1,0:T(8,128)(2,1)} copy(bf16[1,128,3584]{2,1,0:T(8,128)(2,1)} %bitcast.27) | data formatting | bytes 1835008
  136.5 0.0 copy-done
  136.5 0.9 copy.15
Async XLA Ops:
  134.2 2.3 %copy-start = (bf16[128,3584]{1,0:T(8,128)(2,1)S(1)}, bf16[128,3584]{1,0:T(8,128)(2,1)}, u32[]{:S(2)}) copy-start(bf16[128,3584]{1,0:T(8,128)(2,1)} %get-tuple-element.5) | copy-start | bytes 2752516

commit v4 on v3

--- a/solution.py
+++ b/solution.py
@@ -73,18 +73,19 @@
 def kernel(routes_f, routes_b, weights_f, weights_b, x_ref, g_ref, f_ref, gate, up, down,
            out_f, out_b,
            send, got, left, tall, tall_down, pre, back, hid, dgate, dup,
-           part, home, comb, mine, other, from_other, summed, from_far, final, moved,
+           part, home, comb, mine, other, from_other, summed, relay, from_far, final, moved,
            send_sem, recv_sem, wlocal, wsend, wrecv, shift_send, shift_recv, pass_send, pass_recv,
            rsend, rrecv, rlocal, csend, crecv, zsend, zrecv, osend, orecv, olocal, local_sem):
     pipe, ring, x, core = place()
     sibling = device_of(pipe, ring, x, 1 - core)
-    far = device_of(pipe, ring + 4, x, core)
+    up_two = device_of(pipe, ring + 2, x, core)
+    down_two = device_of(pipe, ring - 2, x, core)
     after = device_of(pipe + 1, ring, x, core)
     before = device_of(pipe - 1, ring, x, core)
     tokens, width = x_ref.shape
     quarter = width // 4
     groups = width // GROUP
-    cuts = [groups * i // CHUNKS for i in range(CHUNKS + 1)]
+    cuts = [0, 5, groups]
     hidden = gate.shape[1]
     barrier = pltpu.get_barrier_semaphore()
 
@@ -99,7 +100,7 @@
         if instead is not None:
             pl.when(core == 0)(instead)
 
-    for who in (sibling, far, after, before):
+    for who in (sibling, up_two, down_two, after, before):
         greet(who)
     for k in range(BLOCKS):
         unless_self(k, lambda: greet(source_of(k)))
@@ -185,14 +186,14 @@
         for k in FAR_FIRST:
             unless_self(k, lambda: outward(t, k).wait(), lambda: own_outward(t).wait())
 
-    pl.semaphore_wait(barrier, 2 * BLOCKS + 2 + 2 * core)
+    codes = [code_rows(routes) for routes in (routes_b, routes_f)]
+    build(0, codes[B], x_ref)
+    pl.semaphore_wait(barrier, 2 * BLOCKS + 3 + 2 * core)
     shift(1).start()
     shift(2).start()
+    send_out(0)
     for i in range(3):
         weight(i).start()
-    codes = [code_rows(routes) for routes in (routes_b, routes_f)]
-    build(0, codes[B], x_ref)
-    send_out(0)
     for t in (1, 2):
         shift(t).wait()
         pass_on(t).start()
@@ -337,10 +338,27 @@
             src_ref=other.at[r, :, span_of(n)], dst_ref=from_other.at[r, :, span_of(n)],
             send_sem=csend.at[r, n], recv_sem=crecv.at[r, n], device_id=sibling, device_id_type=MESH)
 
-    def along(r, n):
-        return pltpu.make_async_remote_copy(
-            src_ref=summed.at[r, :, span_of(n)], dst_ref=from_far.at[r, :, span_of(n)],
-            send_sem=zsend.at[r, n], recv_sem=zrecv.at[r, n], device_id=far, device_id_type=MESH)
+    def leg(r, n, way, first):
+        rows = pl.ds(way * half // 2, half // 2)
+        src, dst = (summed, relay) if first else (relay, from_far)
+        stage = 0 if first else 1
+        return pltpu.make_async_remote_copy(
+            src_ref=src.at[r, rows, span_of(n)], dst_ref=dst.at[r, rows, span_of(n)],
+            send_sem=zsend.at[stage, r, n, way], recv_sem=zrecv.at[stage, r, n, way],
+            device_id=(up_two, down_two)[way], device_id_type=MESH)
+
+    def start_along(r, n):
+        for way in range(2):
+            leg(r, n, way, True).start()
+
+    def pass_along(r, n):
+        for way in range(2):
+            leg(r, n, way, True).wait()
+            leg(r, n, way, False).start()
+
+    def wait_along(r, n):
+        for way in range(2):
+            leg(r, n, way, False).wait()
 
     def my_result(r, n):
         return (out_b, out_f)[r].at[pl.ds(half_of(core), half), span_of(n)]
@@ -368,33 +386,50 @@
             return 0
         lax.fori_loop(cuts[n], cuts[n + 1], step, 0)
 
-    def gather(r):
-        for n in range(CHUNKS):
-            wait_home(r, n)
-            combine(r, n, 1 - core, other)
-            across(r, n).start()
-            combine(r, n, core, mine)
-            span = span_of(n)
-            across(r, n).wait()
-            summed[r, :, span] = (mine[r, :, span] + from_other[r, :, span].astype(F32)).astype(BF16)
-            along(r, n).start()
-
-    def finish(r):
-        for n in range(CHUNKS):
-            span = span_of(n)
-            along(r, n).wait()
-            final[r, :, span] = (summed[r, :, span].astype(F32) + from_far[r, :, span].astype(F32)).astype(BF16)
-            result(r, n).start()
-            result_here(r, n).start()
-
-    gather(B)
-    gather(F)
-    finish(B)
-    finish(F)
-    for r in (B, F):
-        for n in range(CHUNKS):
-            result(r, n).wait()
-            result_here(r, n).wait()
+    def gather(r, n):
+        wait_home(r, n)
+        combine(r, n, 1 - core, other)
+        across(r, n).start()
+        combine(r, n, core, mine)
+        span = span_of(n)
+        across(r, n).wait()
+        summed[r, :, span] = (mine[r, :, span] + from_other[r, :, span].astype(F32)).astype(BF16)
+
+    def finish(r, n):
+        span = span_of(n)
+        wait_along(r, n)
+        final[r, :, span] = (summed[r, :, span].astype(F32) + from_far[r, :, span].astype(F32)).astype(BF16)
+        result(r, n).start()
+        result_here(r, n).start()
+
+    order = [(r, n) for r in (B, F) for n in range(CHUNKS)]
+    for i, piece in enumerate(order):
+        gather(*piece)
+        start_along(*piece)
+        if i >= 1:
+            pass_along(*order[i - 1])
+    pass_along(*order[-1])
+    for piece in order:
+        finish(*piece)
+    for piece in order:
+        result(*piece).wait()
+        result_here(*piece).wait()
+
+
+def place_kernel(a, b, out_a, out_b, hold, sem):
+    half = hold.shape[1] // 2
+    pieces = [(i, pl.ds(h * half, half), src, dst) for i, (src, dst) in enumerate(((a, out_a), (b, out_b))) for h in range(2)]
+    reads = [pltpu.make_async_copy(src.at[rows], hold.at[i, rows], sem.at[0, n])
+             for n, (i, rows, src, dst) in enumerate(pieces)]
+    writes = [pltpu.make_async_copy(hold.at[i, rows], dst.at[rows], sem.at[1, n])
+              for n, (i, rows, src, dst) in enumerate(pieces)]
+    for read in reads:
+        read.start()
+    for read, write in zip(reads, writes):
+        read.wait()
+        write.start()
+    for write in writes:
+        write.wait()
 
 
 def body(fwd_in, fwd_routes, fwd_weights, bwd_saved, bwd_grad, bwd_routes, bwd_weights,
@@ -422,17 +457,25 @@
             pltpu.VMEM((ALL, 2 * hidden), BF16),
             pltpu.VMEM((2,) + packed, BF16), pltpu.VMEM((2,) + packed, BF16),
             pltpu.VMEM((2, 5, 2 * tokens, ROWS), BF16),
-            pltpu.VMEM(half, F32)] + [pltpu.VMEM(half, BF16)] * 5 + [
+            pltpu.VMEM(half, F32)] + [pltpu.VMEM(half, BF16)] * 6 + [
             pltpu.VMEM((2, tokens, width), BF16),
             dma((3, BLOCKS)), dma((3, BLOCKS)), dma((3,)), dma((3,)), dma((3,)),
             dma((2,)), dma((2,)), dma((2,)), dma((2,)),
             dma((2, CHUNKS, BLOCKS)), dma((2, CHUNKS, BLOCKS)), dma((2, CHUNKS)),
-            dma((2, CHUNKS)), dma((2, CHUNKS)), dma((2, CHUNKS)), dma((2, CHUNKS)),
+            dma((2, CHUNKS)), dma((2, CHUNKS)), dma((2, 2, CHUNKS, 2)), dma((2, 2, CHUNKS, 2)),
             dma((2, CHUNKS)), dma((2, CHUNKS)), dma((2, CHUNKS)), dma((3,))],
         compiler_params=pltpu.CompilerParams(
             collective_id=0, has_side_effects=True, vmem_limit_bytes=VMEM_LIMIT),
     )(fwd_routes[0].T, bwd_routes[0].T, fwd_weights[0].T, bwd_weights[0].T, bwd_saved[0], bwd_grad[0], fwd_in[0],
       expert_gate[0, 0], expert_up[0, 0], expert_down[0, 0])
+    out_f, out_b = pl.pallas_call(
+        place_kernel,
+        name="place",
+        out_shape=(shape, shape),
+        in_specs=[hbm, hbm],
+        out_specs=(hbm, hbm),
+        scratch_shapes=[pltpu.VMEM((2, tokens, width), BF16), dma((2, 4))],
+    )(out_f, out_b)
     return out_f[None], out_b[None]
 
 

time: 138 us -> 126 us (0.913)
  the two profiles are of different devices: /device:TPU:41 before, /device:TPU:3 now
where the time goes in v4:
time: 126 us; the launch traced here: 125 us
  Pallas kernels  125 us (99%)
    pallas_call x1, Pallas kernels, body(): pl.pallas_call(kernel, name='experts', out_shape=(shape, shape), in_specs...  122 us

profile of v4, /device:TPU:3, one launch (start us, length us, event | category | flops | bytes accessed | tf_op | source)
XLA Modules:
  0.0 125.4 jit_solution(18283429142990344909)
XLA Ops:
  0.6 122.5 %experts.1 = (bf16[128,3584]{1,0:T(8,128)(2,1)}, bf16[128,3584]{1,0:T(8,128)(2,1)}) custom-call(s32[2,128]{1,0:T(2,128)} %bitcast.26, s32[2,128]{1,0:T(2,128)} %bitcast.27, f32[2,128]{1,0:T(2,128)} %bitcast.28, f32[2,128]{1,0:T(2,128)} %bitcast.29, bf16[128,3584]{1,0:T(8,128)(2,1)} %bitcast.23, bf16[128,3584]{1,0:T(8,128)(2,1)} %bitcast.24, ...), custom_call_target="tpu_custom_call" | custom-call | tf_op jit(solution)/shard_map/experts/pallas_call | solution.py:445
  123.1 2.3 %place.1 = (bf16[128,3584]{1,0:T(8,128)(2,1)}, bf16[128,3584]{1,0:T(8,128)(2,1)}) custom-call(bf16[128,3584]{1,0:T(8,128)(2,1)} %get-tuple-element.6.a, bf16[128,3584]{1,0:T(8,128)(2,1)} %get-tuple-element.7.b), custom_call_target="tpu_custom_call" | custom-call | tf_op jit(solution)/shard_map/place/pallas_call | solution.py:471

commit v5 on v4

--- a/solution.py
+++ b/solution.py
@@ -78,14 +78,14 @@
            rsend, rrecv, rlocal, csend, crecv, zsend, zrecv, osend, orecv, olocal, local_sem):
     pipe, ring, x, core = place()
     sibling = device_of(pipe, ring, x, 1 - core)
-    up_two = device_of(pipe, ring + 2, x, core)
-    down_two = device_of(pipe, ring - 2, x, core)
+    onward = device_of(pipe, ring + 2 - 4 * core, x, core)
+    behind = device_of(pipe, ring - 2 + 4 * core, x, core)
     after = device_of(pipe + 1, ring, x, core)
     before = device_of(pipe - 1, ring, x, core)
     tokens, width = x_ref.shape
     quarter = width // 4
     groups = width // GROUP
-    cuts = [0, 5, groups]
+    cuts = [0, 4, groups]
     hidden = gate.shape[1]
     barrier = pltpu.get_barrier_semaphore()
 
@@ -100,7 +100,7 @@
         if instead is not None:
             pl.when(core == 0)(instead)
 
-    for who in (sibling, up_two, down_two, after, before):
+    for who in (sibling, behind, after, before):
         greet(who)
     for k in range(BLOCKS):
         unless_self(k, lambda: greet(source_of(k)))
@@ -188,7 +188,7 @@
 
     codes = [code_rows(routes) for routes in (routes_b, routes_f)]
     build(0, codes[B], x_ref)
-    pl.semaphore_wait(barrier, 2 * BLOCKS + 3 + 2 * core)
+    pl.semaphore_wait(barrier, 2 * BLOCKS + 2 + 2 * core)
     shift(1).start()
     shift(2).start()
     send_out(0)
@@ -338,27 +338,23 @@
             src_ref=other.at[r, :, span_of(n)], dst_ref=from_other.at[r, :, span_of(n)],
             send_sem=csend.at[r, n], recv_sem=crecv.at[r, n], device_id=sibling, device_id_type=MESH)
 
-    def leg(r, n, way, first):
-        rows = pl.ds(way * half // 2, half // 2)
+    def leg(r, n, first):
         src, dst = (summed, relay) if first else (relay, from_far)
         stage = 0 if first else 1
         return pltpu.make_async_remote_copy(
-            src_ref=src.at[r, rows, span_of(n)], dst_ref=dst.at[r, rows, span_of(n)],
-            send_sem=zsend.at[stage, r, n, way], recv_sem=zrecv.at[stage, r, n, way],
-            device_id=(up_two, down_two)[way], device_id_type=MESH)
+            src_ref=src.at[r, :, span_of(n)], dst_ref=dst.at[r, :, span_of(n)],
+            send_sem=zsend.at[stage, r, n], recv_sem=zrecv.at[stage, r, n],
+            device_id=onward, device_id_type=MESH)
 
     def start_along(r, n):
-        for way in range(2):
-            leg(r, n, way, True).start()
+        leg(r, n, True).start()
 
     def pass_along(r, n):
-        for way in range(2):
-            leg(r, n, way, True).wait()
-            leg(r, n, way, False).start()
+        leg(r, n, True).wait()
+        leg(r, n, False).start()
 
     def wait_along(r, n):
-        for way in range(2):
-            leg(r, n, way, False).wait()
+        leg(r, n, False).wait()
 
     def my_result(r, n):
         return (out_b, out_f)[r].at[pl.ds(half_of(core), half), span_of(n)]
@@ -403,14 +399,17 @@
         result_here(r, n).start()
 
     order = [(r, n) for r in (B, F) for n in range(CHUNKS)]
-    for i, piece in enumerate(order):
-        gather(*piece)
-        start_along(*piece)
-        if i >= 1:
-            pass_along(*order[i - 1])
-    pass_along(*order[-1])
-    for piece in order:
-        finish(*piece)
+    for r in (B, F):
+        for n in range(CHUNKS):
+            gather(r, n)
+            start_along(r, n)
+        for n in range(CHUNKS):
+            pass_along(r, n)
+        if r == F:
+            for n in range(CHUNKS):
+                finish(B, n)
+    for n in range(CHUNKS):
+        finish(F, n)
     for piece in order:
         result(*piece).wait()
         result_here(*piece).wait()
@@ -462,7 +461,7 @@
             dma((3, BLOCKS)), dma((3, BLOCKS)), dma((3,)), dma((3,)), dma((3,)),
             dma((2,)), dma((2,)), dma((2,)), dma((2,)),
             dma((2, CHUNKS, BLOCKS)), dma((2, CHUNKS, BLOCKS)), dma((2, CHUNKS)),
-            dma((2, CHUNKS)), dma((2, CHUNKS)), dma((2, 2, CHUNKS, 2)), dma((2, 2, CHUNKS, 2)),
+            dma((2, CHUNKS)), dma((2, CHUNKS)), dma((2, 2, CHUNKS)), dma((2, 2, CHUNKS)),
             dma((2, CHUNKS)), dma((2, CHUNKS)), dma((2, CHUNKS)), dma((3,))],
         compiler_params=pltpu.CompilerParams(
             collective_id=0, has_side_effects=True, vmem_limit_bytes=VMEM_LIMIT),

time: 126 us -> 126 us (level)
  no operation moved by 1% of the time
where the time goes in v5:
time: 126 us; the launch traced here: 124 us
  Pallas kernels  124 us (98%)
    pallas_call x1, Pallas kernels, body(): pl.pallas_call(kernel, name='experts', out_shape=(shape, shape), in_specs...  121 us

profile of v5, /device:TPU:3, one launch (start us, length us, event | category | flops | bytes accessed | tf_op | source)
XLA Modules:
  0.0 124.4 jit_solution(1719385746406342055)
XLA Ops:
  0.6 121.4 %experts.1 = (bf16[128,3584]{1,0:T(8,128)(2,1)}, bf16[128,3584]{1,0:T(8,128)(2,1)}) custom-call(s32[2,128]{1,0:T(2,128)} %bitcast.26, s32[2,128]{1,0:T(2,128)} %bitcast.27, f32[2,128]{1,0:T(2,128)} %bitcast.28, f32[2,128]{1,0:T(2,128)} %bitcast.29, bf16[128,3584]{1,0:T(8,128)(2,1)} %bitcast.23, bf16[128,3584]{1,0:T(8,128)(2,1)} %bitcast.24, ...), custom_call_target="tpu_custom_call" | custom-call | tf_op jit(solution)/shard_map/experts/pallas_call | solution.py:444
  122.1 2.3 %place.1 = (bf16[128,3584]{1,0:T(8,128)(2,1)}, bf16[128,3584]{1,0:T(8,128)(2,1)}) custom-call(bf16[128,3584]{1,0:T(8,128)(2,1)} %get-tuple-element.6.a, bf16[128,3584]{1,0:T(8,128)(2,1)} %get-tuple-element.7.b), custom_call_target="tpu_custom_call" | custom-call | tf_op jit(solution)/shard_map/place/pallas_call | solution.py:470

commit v6 on v4

--- a/solution.py
+++ b/solution.py
@@ -11,7 +11,7 @@
 
 BLOCKS = 8
 STEP_Z = (0, 0, 1, 1, 2, -2, -1, -1)
-FAR_FIRST = (4, 5, 2, 3, 6, 7, 1, 0)
+FAR_FIRST = (4, 5, 2, 6, 3, 7, 1, 0)
 CODE = 32
 ROWS = BLOCKS * 16
 SPARE = BLOCKS * 4
@@ -44,18 +44,18 @@
 
 def target_of(k):
     pipe, ring, x, core = place()
-    return device_of(pipe, ring + STEP_Z[k], x + step_x(k, core), core)
+    return device_of(pipe, ring + STEP_Z[k] * (1 - 2 * core), x + step_x(k, core), core)
 
 
 def source_of(k):
     pipe, ring, x, core = place()
-    return device_of(pipe, ring - STEP_Z[k], x - step_x(k, core), core)
+    return device_of(pipe, ring - STEP_Z[k] * (1 - 2 * core), x - step_x(k, core), core)
 
 
 def expert_of_block(b):
     _, ring, x, core = place()
     away = b >> 1
-    return (((ring + away) & 3) << 2) + ((x + ((b & 1) << 1) + ((away + core) & 1)) & 3)
+    return (((ring + away * (1 - 2 * core)) & 3) << 2) + ((x + ((b & 1) << 1) + ((away + core) & 1)) & 3)
 
 
 def dot(a, b):

time: 126 us -> 127 us (level)
  no operation moved by 1% of the time
where the time goes in v6:
time: 127 us; the launch traced here: 126 us
  Pallas kernels  126 us (99%)
    pallas_call x1, Pallas kernels, body(): pl.pallas_call(kernel, name='experts', out_shape=(shape, shape), in_specs...  123 us

profile of v6, /device:TPU:3, one launch (start us, length us, event | category | flops | bytes accessed | tf_op | source)
XLA Modules:
  0.0 126.3 jit_solution(17396395972927665540)
XLA Ops:
  0.6 123.3 %experts.1 = (bf16[128,3584]{1,0:T(8,128)(2,1)}, bf16[128,3584]{1,0:T(8,128)(2,1)}) custom-call(s32[2,128]{1,0:T(2,128)} %bitcast.26, s32[2,128]{1,0:T(2,128)} %bitcast.27, f32[2,128]{1,0:T(2,128)} %bitcast.28, f32[2,128]{1,0:T(2,128)} %bitcast.29, bf16[128,3584]{1,0:T(8,128)(2,1)} %bitcast.23, bf16[128,3584]{1,0:T(8,128)(2,1)} %bitcast.24, ...), custom_call_target="tpu_custom_call" | custom-call | tf_op jit(solution)/shard_map/experts/pallas_call | solution.py:445
  124.0 2.3 %place.1 = (bf16[128,3584]{1,0:T(8,128)(2,1)}, bf16[128,3584]{1,0:T(8,128)(2,1)}) custom-call(bf16[128,3584]{1,0:T(8,128)(2,1)} %get-tuple-element.6.a, bf16[128,3584]{1,0:T(8,128)(2,1)} %get-tuple-element.7.b), custom_call_target="tpu_custom_call" | custom-call | tf_op jit(solution)/shard_map/place/pallas_call | solution.py:471
